TPU v7x, 512 devices: a whole 4x8x8 slice. The times are simulated.
512 devices in a mesh: win: 32 (over y, z_lo, core), grp: 16 (over x, z_hi).
Axes of the slice: x: 4, y: 8, z: 8 (z_hi: 4, z_lo: 2; z = z_hi * 2 + z_lo), core: 2. Of those that a mesh axis runs over, the one named last changes fastest.
Arguments:
- spectra: bfloat16 [32, 4096, 2, 2048], P(None, 'win', None, 'grp'), may hold values from -6 to 6
- freq_bins: int32 [32], replicated, may hold values from 8 to 39
- slowness: float32 [4], replicated, may hold values from 0.04 to 0.12
- positions: int32 [2048], replicated, may hold values from 0 to 2047, each once
Outputs:
- image: float32 [32, 4, 2048], P('win', None, 'grp')
Inputs may be any that keep to these rules, and one draw needn't show every extreme that they name: `positions`: every grid cell holds exactly one receiver.
All inputs are finite; a program needn't handle non-finite values.
Results may differ from a plain program's by a relative error of at most 0.0003.
Values may be sent and summed in bfloat16 or wider, within the bound.
A program may use at most 64 MiB of HBM per device.

v0:
```python
import math

import jax
import jax.numpy as jnp
from jax import lax
from jax.sharding import PartitionSpec as P

GX = 32
SRC_DEV = 4


HIGHEST_PRECISION = lax.Precision.HIGHEST


def dft_tables(length):
    indices = jnp.arange(length, dtype=jnp.int32)
    products = indices[:, None] * indices[None, :] % length
    phases = products.astype(jnp.float32) * (2.0 * math.pi / length)
    return (jnp.cos(phases), jnp.sin(phases))


def wave_squares(grid_x, grid_y):
    x_index = jnp.arange(grid_x, dtype=jnp.int32)
    y_index = jnp.arange(grid_y, dtype=jnp.int32)
    x_signed = jnp.where(x_index < (grid_x + 1) // 2, x_index, x_index - grid_x).astype(
        jnp.float32
    ) * (2.0 * math.pi / grid_x)
    y_signed = jnp.where(y_index < (grid_y + 1) // 2, y_index, y_index - grid_y).astype(
        jnp.float32
    ) * (2.0 * math.pi / grid_y)
    return x_signed[:, None] ** 2 + y_signed[None, :] ** 2


def along_y(field, table):
    return jnp.einsum("kxy,yv->kxv", field, table, precision=HIGHEST_PRECISION)


def along_x(table, field):
    return jnp.einsum("ux,kxv->kuv", table, field, precision=HIGHEST_PRECISION)


def migrate(field_re, field_im, wavenumber, positions, grid_x):
    shot_count, cell_count = field_re.shape
    grid_y = cell_count // grid_x
    grid_re = (
        jnp.zeros_like(field_re).at[:, positions].set(field_re).reshape(shot_count, grid_x, grid_y)
    )
    grid_im = (
        jnp.zeros_like(field_im).at[:, positions].set(field_im).reshape(shot_count, grid_x, grid_y)
    )
    cos_x, sin_x = dft_tables(grid_x)
    cos_y, sin_y = dft_tables(grid_y)
    section_re = along_y(grid_re, cos_y) + along_y(grid_im, sin_y)
    section_im = along_y(grid_im, cos_y) - along_y(grid_re, sin_y)
    spec_re = along_x(cos_x, section_re) + along_x(sin_x, section_im)
    spec_im = along_x(cos_x, section_im) - along_x(sin_x, section_re)
    squares = wave_squares(grid_x, grid_y)
    factor = 1.0 / math.sqrt(grid_x * grid_y)
    energies = []
    for depth_step in range(wavenumber.shape[0]):
        excess = wavenumber[depth_step] ** 2 - squares
        vertical = jnp.sqrt(jnp.maximum(excess, 0.0))
        damping = jnp.exp(-jnp.sqrt(jnp.maximum(-excess, 0.0)))
        shift_re = damping * jnp.cos(vertical)
        shift_im = damping * jnp.sin(vertical)
        spec_re, spec_im = (
            spec_re * shift_re - spec_im * shift_im,
            spec_re * shift_im + spec_im * shift_re,
        )
        back_re = along_y(spec_re, cos_y) - along_y(spec_im, sin_y)
        back_im = along_y(spec_im, cos_y) + along_y(spec_re, sin_y)
        picture = (along_x(cos_x, back_re) - along_x(sin_x, back_im)) * factor
        energies.append((picture * picture).reshape(shot_count, cell_count))
    return jnp.stack(energies, axis=1)


def body(spectra, freq_bins, slowness, positions):
    freq_count, win_rows, _, receiver_block = spectra.shape
    stride = receiver_block // SRC_DEV
    picked = spectra[:, :, :, ::stride]
    sources = lax.all_gather(picked, "grp", axis=3, tiled=True)
    source_count = sources.shape[3]
    windows = win_rows * lax.axis_size("win")
    source_rows = sources.reshape(freq_count, win_rows, 2 * source_count)
    receiver_rows = spectra.reshape(freq_count, win_rows, 2 * receiver_block)
    wavenumbers = freq_bins.astype(jnp.float32)[:, None] * slowness[None, :]
    factor = 1.0 / source_count
    products = jnp.einsum(
        "fwa,fwb->fab", source_rows, receiver_rows, preferred_element_type=jnp.float32
    )
    real_real = products[:, :source_count, :receiver_block]
    real_imag = products[:, :source_count, receiver_block:]
    imag_real = products[:, source_count:, :receiver_block]
    imag_imag = products[:, source_count:, receiver_block:]
    owned_gram = (
        lax.psum_scatter(
            jnp.stack([real_real + imag_imag, real_imag - imag_real], axis=1),
            "win",
            scatter_dimension=0,
            tiled=True,
        )
        / windows
    )
    freq_index = lax.axis_index("win")
    wavenumber = wavenumbers[freq_index]
    shaped = owned_gram.reshape(2, lax.axis_size("grp"), SRC_DEV, receiver_block)
    received = lax.all_to_all(shaped, "grp", split_axis=1, concat_axis=3, tiled=True)
    images = migrate(received[0, 0], received[1, 0], wavenumber, positions, GX)
    local_image = jnp.sum(images, axis=0)
    own_block = lax.psum_scatter(local_image, "grp", scatter_dimension=1, tiled=True)
    return (own_block * factor)[None]


def solution(mesh):
    return jax.shard_map(
        body,
        mesh=mesh,
        in_specs=(P(None, "win", None, "grp"), P(), P(), P()),
        out_specs=P("win", None, "grp"),
        check_vma=False,
    )
```

profile of v0, /device:TPU:6, one launch (start us, length us, event | category | flops | bytes accessed | tf_op | source)
XLA Modules:
  0.0 520.5 jit_solution(12470274408411681060)
XLA Ops:
  6.5 69.7 %slice.39 = bf16[32,128,2,4]{3,2,1,0:T(2,128)(2,1)S(1)} slice(bf16[32,128,2,128]{3,2,1,0:T(2,128)(2,1)} %param.4), slice={[0:32:1], [0:128:1], [0:2:1], [0:128:32]} | slice | bytes 131072 | tf_op jit(solution)/shard_map/slice | solution.py:80
  76.3 2.1 copy.32
  78.5 3.2 reshape.315
  81.7 59.7 %all-gather.2.cloned.1.call-done = bf16[32,128,2,64]{1,0,2,3:T(8,128)(2,1)} async-done(((bf16[32,128,2,4]{1,0,2,3:T(8,128)(2,1)}), bf16[32,128,2,64]{1,0,2,3:T(8,128)(2,1)}) %all-gather.2.cloned.1.call-update) | async-done | bytes 1048592 | tf_op jit(solution)/shard_map/all_gather | solution.py:81
  141.3 1.9 copy.20
  143.2 0.7 fusion.295
  144.2 1.5 pad_maximum_fusion
  145.7 0.6 copy-done.1
  146.3 0.6 dynamic-slice.2
  146.9 0.6 broadcast_multiply_fusion
  147.6 0.6 fusion.294
  153.1 1.3 dynamic-slice
  154.4 0.4 fusion.69
  154.7 224.1 %all-reduce.3.cloned.1.call-done = f32[32,2,64,128]{3,2,0,1:T(8,128)} async-done(((f32[32,2,64,128]{3,2,0,1:T(8,128)}), f32[32,2,64,128]{3,2,0,1:T(8,128)}) %all-reduce.3.cloned.1.call-update) | async-done | bytes 2097168
  378.9 1.5 dynamic-slice_multiply_fusion
  380.3 0.6 copy.21
  381.0 10.0 %all-to-all-start = ((f32[2,16,4,128]{3,2,0,1:T(4,128)}), f32[2,16,4,128]{3,2,0,1:T(4,128)S(1)}, u32[]{:S(2)}, u32[]{:S(2)}) async-start(f32[2,16,4,128]{3,2,0,1:T(4,128)} %copy.21), calls=%async_computation | async-start | bytes 131072 | tf_op jit(solution)/shard_map/all_to_all | solution.py:107
  391.0 8.1 %all-to-all-done = f32[2,16,4,128]{3,2,0,1:T(4,128)S(1)} async-done(((f32[2,16,4,128]{3,2,0,1:T(4,128)}), f32[2,16,4,128]{3,2,0,1:T(4,128)S(1)}, u32[]{:S(2)}, u32[]{:S(2)}) %all-to-all-start) | async-done | bytes 65568 | tf_op jit(solution)/shard_map/all_to_all | solution.py:107
  399.2 0.4 copy.24
  399.5 5.8 %scatter_custom_fusion.1 = f32[4,2048]{0,1:T(8,128)S(1)} fusion(s32[2048]{0:T(1024)S(1)} %compare_select_fusion, f32[2048,4]{1,0:T(8,128)S(1)} %copy.24, f32[]{:T(128)} %constant.21.clone.1), kind=kCustom, calls=%fused_computation.37 | custom fusion | bytes 32772 | tf_op jit(solution)/shard_map/scatter | solution.py:49
  405.4 0.4 copy.25
  405.8 0.3 fusion.49
  406.1 0.4 copy.22
  406.5 6.0 %scatter_custom_fusion = f32[4,2048]{0,1:T(8,128)S(1)} fusion(s32[2048]{0:T(1024)S(1)} %compare_select_fusion, f32[2048,4]{1,0:T(8,128)S(1)} %copy.22, f32[]{:T(128)} %constant.21.clone.1), kind=kCustom, calls=%fused_computation.39 | custom fusion | bytes 32772 | tf_op jit(solution)/shard_map/scatter | solution.py:46
  412.5 0.4 copy.23
  412.9 0.3 fusion.51
  413.2 0.3 convolution_subtract_fusion.9
  413.6 0.3 convolution_add_fusion.5
  415.1 0.3 fusion.41
  415.4 0.3 fusion.43
  415.8 0.3 fusion.37
  416.1 0.3 fusion.39
  416.5 0.3 fusion.33
  416.8 0.3 fusion.35
  417.2 0.3 fusion.45
  417.5 0.3 fusion.47
  417.9 0.3 convolution_add_fusion.3
  418.2 0.3 convolution_subtract_fusion.7
  419.2 0.3 convolution_add_fusion.2
  419.5 0.3 convolution_subtract_fusion.5
  420.5 0.3 convolution_add_fusion.1
  420.9 0.3 convolution_subtract_fusion.3
  421.9 0.3 convolution_add_fusion
  422.2 0.3 convolution_subtract_fusion.1
  423.3 1.3 copy.30
  424.7 87.7 %reduce-scatter.7.cloned.1.call-done = f32[128,4]{1,0:T(8,128)} async-done(((f32[2048,4]{1,0:T(8,128)}), f32[128,4]{1,0:T(8,128)}) %reduce-scatter.7.cloned.1.call-update) | async-done | bytes 2064
  512.4 0.9 copy.31
  513.3 0.6 multiply_bitcast_fusion
  (35 shorter events, 4.3 us)
Async XLA Ops:
  6.5 134.8 %all-gather.2.cloned.1.call-start = ((), (), s32[]{:S(2)}) async-start(), calls=%async_computation.2 | async-start | bytes 1114112 | tf_op jit(solution)/shard_map/all_gather | solution.py:81
  78.4 300.4 %all-reduce.3.cloned.1.call-start = ((), (), s32[]{:S(2)}) async-start(), calls=%async_computation.4 | async-start | bytes 4194304
  145.7 0.7 copy-start.1
  145.7 1.2 copy-start.2
  145.7 245.3 %copy-start = (s32[2048]{0:T(1024)S(1)}, s32[2048]{0:T(1024)}, u32[]{:S(2)}) copy-start(s32[2048]{0:T(1024)} %param.7) | copy-start | bytes 24580
  381.0 18.2 %all-to-all-start = ((f32[2,16,4,128]{3,2,0,1:T(4,128)}), f32[2,16,4,128]{3,2,0,1:T(4,128)S(1)}, u32[]{:S(2)}, u32[]{:S(2)}) async-start(f32[2,16,4,128]{3,2,0,1:T(4,128)} %copy.21), calls=%async_computation | async-start | bytes 131072 | tf_op jit(solution)/shard_map/all_to_all | solution.py:107
  391.0 121.5 %reduce-scatter.7.cloned.1.call-start = ((), (), s32[]{:S(2)}) async-start(), calls=%async_computation.3 | async-start | bytes 1114112
Sparse Core Ops, SparseCore 0:
  78.6 62.6 all-gather.1
  145.8 233.0 all-reduce.2
  424.8 87.5 reduce-scatter.6
where the time goes:
time: 527 us; the launch traced here: 520 us
  waiting for transfers between devices  380 us (72%)
  local copies, waits for them, and re-layouts  96.7 us (18%)
  between operations  18.3 us (3%)
  matrix products  10.8 us (2%)
  starting transfers between devices  10.1 us (2%)
    unnamed x5, waiting for transfers between devices  312 us
    slice x1, local copies, waits for them, and re-layouts, body(): picked = spectra[:, :, :, ::stride]  69.7 us
    all_gather x1, waiting for transfers between devices, body(): sources = lax.all_gather(picked, 'grp', axis=3, tiled=True)  59.7 us
  transfers between devices with their start and end apart: 4, of which 4 were waited for; matrix products, arithmetic and copies ran while one was open for 1% of the time, Pallas kernels for 0%

commit v1 on v0

v1 whole, which is shorter than its diff:
```python
import functools
import math

import jax
import jax.numpy as jnp
import numpy as np
from jax import lax
from jax.experimental import pallas as pl
from jax.experimental.pallas import tpu as pltpu
from jax.sharding import PartitionSpec as P

MESH = pl.DeviceIdType.MESH
GY = 64
LANES = 128
SHOTS = 4
F32, BF16 = jnp.float32, jnp.bfloat16


def split(table):
    high = table.astype(BF16)
    return high, (table - high.astype(F32)).astype(BF16)


def dot(a, b):
    return jnp.dot(a, b, preferred_element_type=F32)


def dot_lanes(a, b):
    return lax.dot_general(a, b, (((1,), (1,)), ((), ())), preferred_element_type=F32)


def dot3(a, b_high, b_low):
    high, low = split(a)
    width = b_high.shape[1]
    both = dot(high, jnp.concatenate([b_high, b_low], axis=1))
    return both[:, :width] + both[:, width:] + dot(low, b_high)


def np_split(table):
    table = table.astype(np.float32)
    high = table.astype(BF16)
    return high, (table - high.astype(np.float32)).astype(BF16)


def tables(grid_x):
    def angles(length):
        index = np.arange(length)
        return (index[:, None] * index[None, :] % length) * (2.0 * math.pi / length)

    cos_x, sin_x = np.cos(angles(grid_x)), np.sin(angles(grid_x))
    cos_y, sin_y = np.cos(angles(GY)), np.sin(angles(GY))
    shots = np.eye(SHOTS)
    block_cos, block_sin = np.kron(shots, cos_x), np.kron(shots, sin_x)
    rows_y = np.concatenate([cos_y, sin_y], axis=0)
    forward_x = np.concatenate([block_cos, block_sin], axis=1)
    inverse_x = np.concatenate([block_cos, -block_sin], axis=1)
    to_re = np.concatenate([cos_y, -sin_y], axis=0)
    to_im = np.concatenate([sin_y, cos_y], axis=0)
    none = np.zeros_like(to_re)
    inverse_y = np.block([[to_re, none, to_im, none], [none, to_re, none, to_im]])
    x_index, y_index = np.arange(grid_x), np.arange(GY)
    x_signed = np.where(x_index < (grid_x + 1) // 2, x_index, x_index - grid_x).astype(np.float32) * np.float32(
        2.0 * math.pi / grid_x
    )
    y_signed = np.where(y_index < (GY + 1) // 2, y_index, y_index - GY).astype(np.float32) * np.float32(
        2.0 * math.pi / GY
    )
    squares = x_signed[:, None] ** 2 + y_signed[None, :] ** 2
    return (
        np.stack(np_split(rows_y)),
        np.stack(np_split(forward_x)),
        np.stack(np_split(inverse_x)),
        np.stack(np_split(inverse_y)),
        np.concatenate([squares, squares], axis=1).astype(np.float32),
    )


def iota(shape, dim):
    return lax.broadcasted_iota(jnp.int32, shape, dim)


def one_hot(condition):
    return jnp.where(condition, 1.0, 0.0).astype(BF16)


def kernel(
    n_grp, n_win, side, windows,
    spectra, positions, freq_bins, slowness, rows_y, forward_x, inverse_x, inverse_y, squares,
    out,
    u, turned, picked, perm_picked, gram, got_gram, tiles, got_tiles, energy, got_energy,
    y_phase, x_mask, shift,
    local_sem, core_sem, ag_send, ag_recv, rs_send, rs_recv, aa_send, aa_recv, en_send, en_recv,
):
    n_freq = n_win // 2
    grid_x = 2 * n_grp
    rows = 2 * windows
    win, grp = lax.axis_index("win"), lax.axis_index("grp")
    core, chip = lax.rem(win, 2), lax.div(win, 2)
    zh, x = lax.rem(grp, side), lax.div(grp, side)
    other = 1 - core

    def peer_chip(d):
        return lax.rem(chip + d, n_freq)

    def device(chip_at, core_at, grp_at):
        return (chip_at * 2 + core_at, grp_at)

    own_copy = pltpu.make_async_copy(spectra.at[:, core], u.at[:, core], local_sem.at[0])
    own_copy.start()

    barrier = pltpu.get_barrier_semaphore()
    pl.semaphore_signal(barrier, inc=1, device_id=device(chip, other, grp), device_id_type=MESH)
    for d in range(1, n_grp):
        pl.semaphore_signal(barrier, inc=1, device_id=device(chip, core, lax.rem(grp + d, n_grp)), device_id_type=MESH)
    for d in range(1, n_freq):
        pl.semaphore_signal(barrier, inc=1, device_id=device(peer_chip(d), core, grp), device_id_type=MESH)
    pl.semaphore_wait(barrier, n_grp + n_freq - 1)

    core_copy = pltpu.make_async_remote_copy(
        src_ref=spectra.at[:, other], dst_ref=u.at[:, core], send_sem=core_sem.at[0], recv_sem=core_sem.at[1],
        device_id=device(chip, other, grp), device_id_type=MESH,
    )
    core_copy.start()
    own_copy.wait()
    core_copy.wait()

    mine = jnp.zeros((n_freq * SHOTS, 2 * rows), F32)
    row, lane = iota((n_freq * SHOTS, LANES), 0), iota((n_freq * SHOTS, LANES), 1)
    for q in range(n_freq):
        pick = one_hot(lane == (row - SHOTS * q) * (LANES // SHOTS))
        mine += dot_lanes(pick, u[q].reshape(2 * rows, LANES))
    picked[grp] = mine.astype(BF16)

    def source_copy(holder, target, slot):
        return pltpu.make_async_remote_copy(
            src_ref=picked.at[holder], dst_ref=picked.at[holder], send_sem=ag_send.at[slot], recv_sem=ag_recv.at[slot],
            device_id=device(chip, core, target), device_id_type=MESH,
        )

    sends = []
    for d in range(1, side):
        sends.append(source_copy(grp, x * side + lax.rem(zh + d, side), d))
        sends[-1].start()
    for e in range(1, side):
        sends.append(source_copy(grp, lax.rem(x + e, side) * side + zh, e * side))
        sends[-1].start()

    row, lane = iota((rows, rows), 0), iota((rows, rows), 1)
    even = lax.rem(row, 2) == 0
    swap = jnp.where(even & (lane == row + 1), 1.0, jnp.where(~even & (lane == row - 1), -1.0, 0.0)).astype(BF16)

    def turn(i, carry):
        for half in range(2):
            turned[i, half] = dot(swap, u[i, half]).astype(BF16)
        return carry

    lax.fori_loop(0, n_freq, turn, 0)

    where = positions[...]
    cell_x, cell_y = lax.shift_right_logical(where, 6), jnp.bitwise_and(where, GY - 1)
    receivers = n_grp * LANES
    y_hot = one_hot(iota((GY, receivers), 0) == cell_y)
    y_phase[0:LANES] = dot(rows_y[0], y_hot).astype(BF16)
    y_phase[LANES:] = dot(rows_y[1], y_hot).astype(BF16)
    x_mask[...] = one_hot(iota((grid_x, receivers), 0) == cell_x)
    freq = freq_bins[win].astype(F32)
    sign = jnp.where(iota((grid_x, LANES), 1) < GY, -1.0, 1.0)
    total_re, total_im = None, None
    for k in range(4):
        kappa = freq * slowness[k]
        excess = kappa * kappa - squares[...]
        vertical = jnp.sqrt(jnp.maximum(excess, 0.0))
        damping = jnp.exp(-jnp.sqrt(jnp.maximum(-excess, 0.0)))
        step_re, step_im = damping * jnp.cos(vertical), damping * jnp.sin(vertical)
        if k == 0:
            total_re, total_im = step_re, step_im
        else:
            total_re, total_im = total_re * step_re - total_im * step_im, total_re * step_im + total_im * step_re
        shift[k, 0] = total_re
        shift[k, 1] = sign * total_im

    for d in range(1, side):
        origin = x * side + lax.rem(zh + side - d, side)
        source_copy(origin, grp, d).wait_recv()
        for e in range(1, side):
            sends.append(source_copy(origin, lax.rem(x + e, side) * side + zh, e * side + d))
            sends[-1].start()
    for e in range(1, side):
        for d in range(side):
            origin = lax.rem(x + side - e, side) * side + lax.rem(zh + side - d, side)
            source_copy(origin, grp, e * side + d).wait_recv()

    group = 16 // SHOTS
    height = 16 * n_grp
    row, lane = iota((height, height), 0), iota((height, height), 1)
    n_src = SHOTS * n_grp
    q_of, src_of = lax.div(row, n_src), lax.rem(row, n_src)
    reorder = one_hot(lane == lax.div(src_of, SHOTS) * 16 + q_of * SHOTS + lax.rem(src_of, SHOTS))
    for a in range(n_freq * SHOTS // 16):
        block = picked[:, 16 * a : 16 * (a + 1), :].reshape(height, 2 * rows)
        perm_picked[group * a : group * (a + 1)] = dot(reorder, block).astype(BF16).reshape(group, n_src, 2 * rows)

    def gram_copy(d):
        return pltpu.make_async_remote_copy(
            src_ref=gram.at[peer_chip(d)], dst_ref=got_gram.at[d], send_sem=rs_send.at[d], recv_sem=rs_recv.at[d],
            device_id=device(peer_chip(d), core, grp), device_id_type=MESH,
        )

    for d in list(range(1, n_freq)) + [0]:
        q = peer_chip(d)
        right = jnp.concatenate([u[q].reshape(2 * rows, LANES), turned[q].reshape(2 * rows, LANES)], axis=1)
        gram[q] = dot(perm_picked[q], right)
        if d:
            sends.append(gram_copy(d))
            sends[-1].start()
    total = gram[chip]
    for d in range(1, n_freq):
        gram_copy(d).wait_recv()
        total += got_gram[d]

    real, imag = total[:, :LANES], total[:, LANES:]
    upper = lax.rem(iota((n_src, LANES), 0), 8) < SHOTS
    first = jnp.where(upper, real, pltpu.roll(imag, SHOTS, 0))
    second = jnp.where(upper, pltpu.roll(real, n_src - SHOTS, 0), imag)
    for a in range(n_grp // 2):
        tiles[2 * a] = first[8 * a : 8 * a + 8]
        tiles[2 * a + 1] = second[8 * a : 8 * a + 8]

    def tile_copy(d):
        target = lax.rem(grp + d, n_grp)
        return pltpu.make_async_remote_copy(
            src_ref=tiles.at[target], dst_ref=got_tiles.at[grp], send_sem=aa_send.at[d], recv_sem=aa_recv.at[d],
            device_id=device(chip, core, target), device_id_type=MESH,
        )

    for d in range(1, n_grp):
        sends.append(tile_copy(d))
        sends[-1].start()
    got_tiles[grp] = tiles[grp]
    for d in range(1, n_grp):
        tile_copy(d).wait_recv()

    field = jnp.concatenate([got_tiles[g] for g in range(n_grp)], axis=1)
    field_high = field.astype(BF16).astype(F32)
    field_low = field - field_high
    mask = x_mask[...]

    def placed(part):
        return jnp.concatenate(
            [jnp.broadcast_to(part[i : i + 1], (grid_x, receivers)).astype(BF16) * mask for i in range(2 * SHOTS)], axis=0
        )

    section = dot_lanes(placed(field_high), y_phase[...])
    section = section[:, :LANES] + section[:, LANES:] + dot_lanes(placed(field_low), y_phase[0:LANES])
    half = SHOTS * grid_x
    lower = iota((half, LANES), 1) < GY
    plus_minus = jnp.where(lower, 1.0, -1.0)
    section = plus_minus * section[:half] + pltpu.roll(section[half:], GY, 1)
    turned_section = plus_minus * pltpu.roll(section, GY, 1)
    stacked = jnp.concatenate([section, turned_section], axis=0)
    stacked_high, stacked_low = split(stacked)
    both = dot(forward_x[0], jnp.concatenate([stacked_high, stacked_low], axis=1))
    spec = both[:, :LANES] + both[:, LANES:] + dot(forward_x[1], stacked_high)
    spec_turned = pltpu.roll(spec, GY, 1)
    spec3, spec3_turned = spec.reshape(SHOTS, grid_x, LANES), spec_turned.reshape(SHOTS, grid_x, LANES)
    for p in range(2):
        shifted = [
            (spec3 * shift[k, 0][None] + spec3_turned * shift[k, 1][None]).reshape(half, LANES) for k in (2 * p, 2 * p + 1)
        ]
        back = dot3(jnp.concatenate(shifted, axis=1), inverse_y[0], inverse_y[1])
        back = jnp.concatenate([back[:, :LANES], back[:, LANES:]], axis=0)
        back_high, back_low = split(back)
        both = dot(inverse_x[0], jnp.concatenate([back_high, back_low], axis=1))
        picture = both[:, :LANES] + both[:, LANES:] + dot(inverse_x[1], back_high)
        energies = jnp.sum((picture * picture).reshape(SHOTS, grid_x, LANES), axis=0)
        for g in range(n_grp):
            energy[g, 2 * p : 2 * p + 2] = energies[2 * g : 2 * g + 2]

    def energy_copy(d):
        target = lax.rem(grp + d, n_grp)
        return pltpu.make_async_remote_copy(
            src_ref=energy.at[target], dst_ref=got_energy.at[d], send_sem=en_send.at[d], recv_sem=en_recv.at[d],
            device_id=device(chip, core, target), device_id_type=MESH,
        )

    for d in range(1, n_grp):
        sends.append(energy_copy(d))
        sends[-1].start()
    image = energy[grp]
    for d in range(1, n_grp):
        energy_copy(d).wait_recv()
        image += got_energy[d]
    n_windows = windows * n_win
    scale = 1.0 / (n_src * grid_x * GY * n_windows * n_windows)
    for p in range(2):
        one, two = image[2 * p : 2 * p + 1] * scale, image[2 * p + 1 : 2 * p + 2] * scale
        low = iota((1, LANES), 1) < GY
        out[2 * p : 2 * p + 1] = jnp.where(low, one, pltpu.roll(two, GY, 1))
        out[2 * p + 1 : 2 * p + 2] = jnp.where(low, pltpu.roll(one, GY, 1), two)

    for copy in sends:
        copy.wait_send()


def body(n_grp, n_win, spectra, freq_bins, slowness, positions):
    freqs, windows, _, block = spectra.shape
    side = math.isqrt(n_grp)
    grid_x = 2 * n_grp
    n_freq = n_win // 2
    rows = 2 * windows
    n_src = SHOTS * n_grp
    receivers = n_grp * block
    hbm, vmem, smem = (pl.BlockSpec(memory_space=m) for m in (pl.ANY, pltpu.VMEM, pltpu.SMEM))
    dma = pltpu.SemaphoreType.DMA
    consts = tables(grid_x)
    image = pl.pallas_call(
        functools.partial(kernel, n_grp, n_win, side, windows),
        out_shape=jax.ShapeDtypeStruct((4, block), F32),
        in_specs=[hbm, vmem, smem, smem] + [vmem] * len(consts),
        out_specs=vmem,
        scratch_shapes=[
            pltpu.VMEM((n_freq, 2, rows, block), BF16),
            pltpu.VMEM((n_freq, 2, rows, block), BF16),
            pltpu.VMEM((n_grp, n_freq * SHOTS, 2 * rows), BF16),
            pltpu.VMEM((n_freq, n_src, 2 * rows), BF16),
            pltpu.VMEM((n_freq, n_src, 2 * block), F32),
            pltpu.VMEM((n_freq, n_src, 2 * block), F32),
            pltpu.VMEM((n_grp, 2 * SHOTS, block), F32),
            pltpu.VMEM((n_grp, 2 * SHOTS, block), F32),
            pltpu.VMEM((n_grp, SHOTS, block), F32),
            pltpu.VMEM((n_grp, SHOTS, block), F32),
            pltpu.VMEM((2 * LANES, receivers), BF16),
            pltpu.VMEM((grid_x, receivers), BF16),
            pltpu.VMEM((4, 2, grid_x, LANES), F32),
            dma((1,)), dma((2,)),
            dma((n_grp,)), dma((n_grp,)), dma((n_freq,)), dma((n_freq,)),
            dma((n_grp,)), dma((n_grp,)), dma((n_grp,)), dma((n_grp,)),
        ],
        compiler_params=pltpu.CompilerParams(
            collective_id=0, has_side_effects=True, vmem_limit_bytes=48 * 1024 * 1024
        ),
    )(
        spectra.reshape(n_freq, 2, rows, block),
        positions.reshape(1, receivers),
        freq_bins,
        slowness,
        *(jnp.asarray(c) for c in consts),
    )
    return image[None]


def solution(mesh):
    return jax.shard_map(
        functools.partial(body, mesh.shape["grp"], mesh.shape["win"]),
        mesh=mesh,
        in_specs=(P(None, "win", None, "grp"), P(), P(), P()),
        out_specs=P("win", None, "grp"),
        check_vma=False,
    )
```

time: 527 us -> 87.3 us (0.17); the launches traced: 520 us -> 86.9 us
  waiting for transfers between devices: 380 us -> 0 us
  local copies, waits for them, and re-layouts: 96.7 us -> 8.49 us
  Pallas kernels: 0 us -> 78.4 us
  between operations: 18.3 us -> 0.02 us
  matrix products: 10.8 us -> 0 us
  starting transfers between devices: 10.1 us -> 0 us
    unnamed x5 -> x0, waiting for transfers between devices: 312 us -> none
    pallas_call x0 -> x1, Pallas kernels: none -> 78.4 us  [body(): pl.pallas_call(functools.partial(kernel, n_grp, n_win, side, windows), ou...]
    slice x2 -> x0, local copies, waits for them, and re-layouts: 70.4 us -> none  [the longest x1 69.7 us: body(): picked = spectra[:, :, :, ::stride]]
    all_gather x1 -> x0, waiting for transfers between devices: 59.7 us -> none  [body(): sources = lax.all_gather(picked, 'grp', axis=3, tiled=True)]
    scatter x2 -> x0, local copies, waits for them, and re-layouts: 11.9 us -> none  [the longest x1 6.03 us: migrate(): jnp.zeros_like(field_re).at[:, positions].set(field_re)]
    dot_general x33 -> x0, matrix products: 10.8 us -> none  [the longest x20 6.74 us: along_y(): return jnp.einsum('kxy,yv->kxv', field, table, precision=HIGHEST_PRECISION)]
    all_to_all x1 -> x0, starting transfers between devices: 9.98 us -> none  [body(): lax.all_to_all(shaped, 'grp', split_axis=1, concat_axis=3, tiled=True)]
    all_to_all x1 -> x0, waiting for transfers between devices: 8.11 us -> none  [body(): lax.all_to_all(shaped, 'grp', split_axis=1, concat_axis=3, tiled=True)]
  transfers between devices with their start and end apart: 4 -> 0, of which waited for: 4 -> 0; matrix products, arithmetic and copies ran while one was open for 1% -> 0% of each run, Pallas kernels for 0% -> 0%
where the time goes in v1:
time: 87.3 us; the launch traced here: 86.9 us
  Pallas kernels  78.4 us (90%)
  local copies, waits for them, and re-layouts  8.49 us (10%)
    pallas_call x1, Pallas kernels, body(): pl.pallas_call(functools.partial(kernel, n_grp, n_win, side, windows), ou...  78.4 us
    unnamed x19, local copies, waits for them, and re-layouts  8.49 us

profile of v1, /device:TPU:6, one launch (start us, length us, event | category | flops | bytes accessed | tf_op | source)
XLA Modules:
  0.0 86.9 jit_solution(7696057521765618403)
XLA Ops:
  0.0 0.0 copy-start
  0.0 1.6 %copy-done = bf16[32,128,2,128]{3,2,1,0:T(2,128)(2,1)S(1)} copy-done((bf16[32,128,2,128]{3,2,1,0:T(2,128)(2,1)S(1)}, bf16[32,128,2,128]{3,2,1,0:T(2,128)(2,1)}, u32[]{:S(2)}) %copy-start) | copy-done | bytes 2097176
  1.6 0.0 copy-start.1
  1.6 0.9 %copy-done.1 = bf16[2,256,256]{2,1,0:T(8,128)(2,1)S(1)} copy-done((bf16[2,256,256]{2,1,0:T(8,128)(2,1)S(1)}, bf16[2,256,256]{2,1,0:T(8,128)(2,1)}, u32[]{:S(2)}) %copy-start.1) | copy-done | bytes 262168
  2.5 0.0 copy-start.2
  2.5 0.9 %copy-done.2 = bf16[2,128,256]{2,1,0:T(8,128)(2,1)S(1)} copy-done((bf16[2,128,256]{2,1,0:T(8,128)(2,1)S(1)}, bf16[2,128,256]{2,1,0:T(8,128)(2,1)}, u32[]{:S(2)}) %copy-start.2) | copy-done | bytes 131096
  3.4 0.0 copy-start.3
  3.4 0.9 %copy-done.3 = bf16[2,128,256]{2,1,0:T(8,128)(2,1)S(1)} copy-done((bf16[2,128,256]{2,1,0:T(8,128)(2,1)S(1)}, bf16[2,128,256]{2,1,0:T(8,128)(2,1)}, u32[]{:S(2)}) %copy-start.3) | copy-done | bytes 131096
  4.4 0.0 copy-start.4
  4.4 0.8 copy-done.4
  5.2 0.0 copy-start.5
  5.2 0.7 copy-done.5
  5.9 0.0 copy-start.6
  5.9 0.7 copy-done.6
  6.6 0.0 copy-start.7
  6.6 0.7 copy-done.7
  7.3 0.0 copy-start.8
  7.3 0.7 copy-done.8
  7.9 78.4 %shard_map.91 = f32[4,128]{1,0:T(4,128)S(1)} custom-call(bf16[16,2,256,128]{3,2,1,0:T(8,128)(2,1)S(1)} %bitcast.3, s32[1,2048]{1,0:T(1,128)S(1)} %bitcast.4, s32[32]{0:T(128)S(1)} %copy-done.7, f32[4]{0:T(128)S(1)} %copy-done.8, bf16[2,128,64]{2,1,0:T(8,128)(2,1)S(1)} %copy-done.4, bf16[2,128,256]{2,1,0:T(8,128)(2,1)S(1)} %copy-done.3, ...), custom_call_target="tpu_custom_call" | custom-call | tf_op jit(solution)/shard_map/pallas_call | solution.py:316
  86.3 0.6 copy.11
Async XLA Ops:
  0.0 1.6 %copy-start = (bf16[32,128,2,128]{3,2,1,0:T(2,128)(2,1)S(1)}, bf16[32,128,2,128]{3,2,1,0:T(2,128)(2,1)}, u32[]{:S(2)}) copy-start(bf16[32,128,2,128]{3,2,1,0:T(2,128)(2,1)} %param.9) | copy-start | bytes 6291460
  1.6 0.9 %copy-start.1 = (bf16[2,256,256]{2,1,0:T(8,128)(2,1)S(1)}, bf16[2,256,256]{2,1,0:T(8,128)(2,1)}, u32[]{:S(2)}) copy-start(bf16[2,256,256]{2,1,0:T(8,128)(2,1)} %constant.13.clone.inverse_y) | copy-start | bytes 786436
  2.5 0.9 %copy-start.2 = (bf16[2,128,256]{2,1,0:T(8,128)(2,1)S(1)}, bf16[2,128,256]{2,1,0:T(8,128)(2,1)}, u32[]{:S(2)}) copy-start(bf16[2,128,256]{2,1,0:T(8,128)(2,1)} %constant.12.clone.inverse_x) | copy-start | bytes 393220
  3.4 0.9 %copy-start.3 = (bf16[2,128,256]{2,1,0:T(8,128)(2,1)S(1)}, bf16[2,128,256]{2,1,0:T(8,128)(2,1)}, u32[]{:S(2)}) copy-start(bf16[2,128,256]{2,1,0:T(8,128)(2,1)} %constant.11.clone.forward_x) | copy-start | bytes 393220
  4.4 0.8 copy-start.4
  5.2 0.7 copy-start.5
  5.9 0.7 copy-start.6
  6.6 0.7 copy-start.7
  7.3 0.7 copy-start.8

commit v2 on v1

v2 whole, which is shorter than its diff:
```python
import functools
import math

import jax
import jax.numpy as jnp
import numpy as np
from jax import lax
from jax.experimental import pallas as pl
from jax.experimental.pallas import tpu as pltpu
from jax.sharding import PartitionSpec as P

MESH = pl.DeviceIdType.MESH
GY = 64
N_X = 4
LANES = 128
SHOTS = 4
F32, BF16 = jnp.float32, jnp.bfloat16


def split(table):
    high = table.astype(BF16)
    return high, (table - high.astype(F32)).astype(BF16)


def dot(a, b):
    return jnp.dot(a, b, preferred_element_type=F32)


def dot_lanes(a, b):
    return lax.dot_general(a, b, (((1,), (1,)), ((), ())), preferred_element_type=F32)


def dot3(a, b_high, b_low):
    high, low = split(a)
    width = b_high.shape[1]
    both = dot(high, jnp.concatenate([b_high, b_low], axis=1))
    return both[:, :width] + both[:, width:] + dot(low, b_high)


def np_split(table):
    table = table.astype(np.float32)
    high = table.astype(BF16)
    return high, (table - high.astype(np.float32)).astype(BF16)


def tables(grid_x):
    def angles(length):
        index = np.arange(length)
        return (index[:, None] * index[None, :] % length) * (2.0 * math.pi / length)

    cos_x, sin_x = np.cos(angles(grid_x)), np.sin(angles(grid_x))
    cos_y, sin_y = np.cos(angles(GY)), np.sin(angles(GY))
    shots = np.eye(SHOTS)
    block_cos, block_sin = np.kron(shots, cos_x), np.kron(shots, sin_x)
    rows_y = np.concatenate([cos_y, sin_y], axis=0)
    forward_x = np.concatenate([block_cos, block_sin], axis=1)
    inverse_x = np.concatenate([block_cos, -block_sin], axis=1)
    to_re = np.concatenate([cos_y, -sin_y], axis=0)
    to_im = np.concatenate([sin_y, cos_y], axis=0)
    none = np.zeros_like(to_re)
    inverse_y = np.block([[to_re, none, to_im, none], [none, to_re, none, to_im]])
    x_index, y_index = np.arange(grid_x), np.arange(GY)
    x_signed = np.where(x_index < (grid_x + 1) // 2, x_index, x_index - grid_x).astype(np.float32) * np.float32(
        2.0 * math.pi / grid_x
    )
    y_signed = np.where(y_index < (GY + 1) // 2, y_index, y_index - GY).astype(np.float32) * np.float32(
        2.0 * math.pi / GY
    )
    squares = x_signed[:, None] ** 2 + y_signed[None, :] ** 2
    return (
        np.stack(np_split(rows_y)),
        np.stack(np_split(forward_x)),
        np.stack(np_split(inverse_x)),
        np.stack(np_split(inverse_y)),
        np.concatenate([squares, squares], axis=1).astype(np.float32),
    )


def iota(shape, dim):
    return lax.broadcasted_iota(jnp.int32, shape, dim)


def one_hot(condition):
    return jnp.where(condition, 1.0, 0.0).astype(BF16)


def kernel(
    n_grp, n_win, windows,
    spectra, positions_hbm, freq_hbm, slowness_hbm, rows_hbm, forward_hbm, inverse_x_hbm, inverse_y_hbm, squares_hbm,
    out,
    positions, freq_bins, slowness, rows_y, forward_x, inverse_x, inverse_y, squares,
    u, v, picked, theirs, gram, got_plus, got_minus, got_z, tiles, got_tiles, energy, got_energy,
    y_phase, x_mask, shift,
    local_sem, core_sem, z_send, z_recv, x_send, x_recv, rs_send, rs_recv, zx_sem, aa_send, aa_recv, en_send, en_recv,
):
    n_freq = n_win // 2
    n_y = n_freq // 2
    n_z = n_grp // N_X
    n_src = SHOTS * n_grp
    grid_x = 2 * n_grp
    receivers = n_grp * LANES
    rows = 2 * windows
    win, grp = lax.axis_index("win"), lax.axis_index("grp")
    core, chip = lax.rem(win, 2), lax.div(win, 2)
    z_low, y = lax.rem(chip, 2), lax.div(chip, 2)
    zh, x = lax.rem(grp, n_z), lax.div(grp, n_z)
    other = 1 - core

    def at_y(d):
        return lax.rem(y + d + n_y, n_y)

    def at_x(d):
        return lax.rem(x + d + N_X, N_X)

    def at_zh(d):
        return lax.rem(zh + d + n_z, n_z)

    def device(chip_at, core_at, grp_at):
        return (chip_at * 2 + core_at, grp_at)

    def remote(src, dst, send_sem, recv_sem, target):
        return pltpu.make_async_remote_copy(
            src_ref=src, dst_ref=dst, send_sem=send_sem, recv_sem=recv_sem, device_id=target, device_id_type=MESH
        )

    sends = []

    def send(copy):
        copy.start()
        sends.append(copy)

    partner = device(chip, other, grp)
    z_partner = device(y * 2 + 1 - z_low, core, grp)
    barrier = pltpu.get_barrier_semaphore()
    greeted = [partner, z_partner, device(at_y(1) * 2 + z_low, core, grp), device(at_y(-1) * 2 + z_low, core, grp)]
    greeted += [device(chip, core, lax.rem(grp + d, n_grp)) for d in range(1, n_grp)]
    for target in greeted:
        pl.semaphore_signal(barrier, inc=1, device_id=target, device_id_type=MESH)

    loads = [
        pltpu.make_async_copy(source, target, local_sem.at[i])
        for i, (source, target) in enumerate(
            (
                (spectra.at[:, core], u.at[:, core]),
                (spectra.at[:, other], v),
                (positions_hbm, positions),
                (freq_hbm, freq_bins),
                (slowness_hbm, slowness),
                (rows_hbm, rows_y),
                (forward_hbm, forward_x),
                (inverse_x_hbm, inverse_x),
                (inverse_y_hbm, inverse_y),
                (squares_hbm, squares),
            )
        )
    ]
    for load in loads:
        load.start()

    ahead = [n_y // 2] + [d for k in range(n_y // 2 - 1, 0, -1) for d in (k, -k)] + [0]
    slots = [(d, z) for d in ahead for z in range(2)]
    chunk = 16 // SHOTS
    n_chunk = n_freq // chunk

    def freq_of(slot):
        return at_y(slots[slot][0]) * 2 + slots[slot][1]

    loads[0].wait()
    loads[1].wait()
    row, lane = iota((n_freq * SHOTS, LANES), 0), iota((n_freq * SHOTS, LANES), 1)
    own = jnp.zeros((n_freq * SHOTS, rows), F32)
    for_partner = jnp.zeros((n_freq * SHOTS, rows), F32)
    for slot in range(n_freq):
        pick = one_hot(lane == (row - SHOTS * slot) * (LANES // SHOTS))
        own += dot_lanes(pick, u[freq_of(slot), core])
        for_partner += dot_lanes(pick, v[freq_of(slot)])
    own, for_partner = own.astype(BF16), for_partner.astype(BF16)
    for c in range(n_chunk):
        picked[c, grp, core] = own[16 * c : 16 * c + 16]
        theirs[c] = for_partner[16 * c : 16 * c + 16]

    pl.semaphore_wait(barrier, len(greeted))

    pick_copy = remote(theirs, picked.at[:, grp, core], core_sem.at[0], core_sem.at[1], partner)
    send(pick_copy)
    core_copy = remote(v, u.at[:, core], core_sem.at[2], core_sem.at[3], partner)
    send(core_copy)
    pick_copy.wait_recv()

    def z_copy(c, d, holder):
        return remote(
            picked.at[c, holder], picked.at[c, holder], z_send.at[c, d], z_recv.at[c, d],
            device(chip, core, x * n_z + at_zh(d)),
        )

    def x_copy(c, holder_x, first, count, step, kind):
        part = pl.ds(holder_x * n_z + first, count)
        sem = 2 * kind + (0 if step > 0 else 1)
        return remote(
            picked.at[c, part], picked.at[c, part], x_send.at[c, sem], x_recv.at[c, sem],
            device(chip, core, at_x(step) * n_z + zh),
        )

    for c in range(n_chunk):
        for d in range(1, n_z):
            send(z_copy(c, d, grp))

    def x_start(c):
        for d in range(1, n_z):
            z_copy(c, d, x * n_z + at_zh(-d)).wait_recv()
        for step in (1, -1):
            send(x_copy(c, x, 0, n_z, step, 0))

    def x_forward(c):
        for step in (1, -1):
            x_copy(c, at_x(-step), 0, n_z, step, 0).wait_recv()
            send(x_copy(c, at_x(-step), 0 if step > 0 else n_z // 2, n_z // 2, step, 1))

    def x_finish(c):
        for step in (1, -1):
            x_copy(c, at_x(-2 * step), 0 if step > 0 else n_z // 2, n_z // 2, step, 1).wait_recv()

    def side_tables():
        for load in loads[2:]:
            load.wait()
        where = positions[...]
        cell_x, cell_y = lax.shift_right_logical(where, 6), jnp.bitwise_and(where, GY - 1)
        y_hot = one_hot(iota((GY, receivers), 0) == cell_y)
        y_phase[0:LANES] = dot(rows_y[0], y_hot).astype(BF16)
        y_phase[LANES:] = dot(rows_y[1], y_hot).astype(BF16)
        x_mask[...] = one_hot(iota((grid_x, receivers), 0) == cell_x)
        freq = freq_bins[win].astype(F32)
        sign = jnp.where(iota((grid_x, LANES), 1) < GY, -1.0, 1.0)
        total_re, total_im = None, None
        for k in range(4):
            kappa = freq * slowness[k]
            excess = kappa * kappa - squares[...]
            vertical = jnp.sqrt(jnp.maximum(excess, 0.0))
            damping = jnp.exp(-jnp.sqrt(jnp.maximum(-excess, 0.0)))
            step_re, step_im = damping * jnp.cos(vertical), damping * jnp.sin(vertical)
            if k == 0:
                total_re, total_im = step_re, step_im
            else:
                total_re, total_im = total_re * step_re - total_im * step_im, total_re * step_im + total_im * step_re
            shift[k, 0] = total_re
            shift[k, 1] = sign * total_im

    height = 16 * n_grp
    row, lane = iota((height, height), 0), iota((height, height), 1)
    slot_of, src_of = lax.div(row, n_src), lax.rem(row, n_src)
    reorder = one_hot(lane == lax.div(src_of, SHOTS) * 16 + slot_of * SHOTS + lax.rem(src_of, SHOTS))
    row, lane = iota((rows, rows), 0), iota((rows, rows), 1)
    even = lax.rem(row, 2) == 0
    turn = jnp.where(~even & (lane == row - 1), -1.0, jnp.where(even & (lane == row + 1), 1.0, 0.0)).astype(BF16)

    def grams(c):
        sources = []
        for half in range(2):
            plain = dot(reorder, picked[c, :, half].reshape(height, rows)).astype(BF16)
            sources.append((plain, dot(plain, turn).astype(BF16)))
        for i in range(chunk):
            slot = chunk * c + i
            q = freq_of(slot)
            result = None
            for half, (plain, turned) in enumerate(sources):
                left = jnp.concatenate([plain[n_src * i : n_src * (i + 1)], turned[n_src * i : n_src * (i + 1)]], axis=0)
                term = dot(left, u[q, half])
                result = term if result is None else result + term
            gram[slot] = result

    def ring_copy(d, z, step):
        slot = slots.index((abs(d) if abs(d) == n_y // 2 else d, z))
        index = (abs(d) - 1) * 2 + z
        got = got_plus if step > 0 else got_minus
        lane_ = 0 if step > 0 else 1
        return remote(
            gram.at[slot], got.at[index], rs_send.at[lane_, index], rs_recv.at[lane_, index],
            device(at_y(step) * 2 + z_low, core, grp),
        )

    def ring_start(d, z, step):
        send(ring_copy(d, z, step))

    def arrived(d, z, step):
        ring_copy(d + step, z, step).wait_recv()
        got = got_plus if step > 0 else got_minus
        return got[(abs(d + step) - 1) * 2 + z]

    def ring_forward(d, z, step):
        slot = slots.index((d, z))
        gram[slot] = gram[slot] + arrived(d, z, step)
        ring_start(d, z, step)

    far = n_y // 2

    def ring(c):
        for place in (2 * c - 1, 2 * c):
            if place < 0:
                continue
            d = ahead[place]
            if d == far:
                ring_start(far, 0, 1)
                ring_start(-far, 1, -1)
                ring_start(far - 1, 1, 1)
            elif d > 0:
                if d == far - 1:
                    ring_forward(d, 0, 1)
                else:
                    ring_forward(d, 1, 1)
                    ring_forward(d, 0, 1)
            elif d < 0:
                if d == 1 - far:
                    ring_start(d, 0, -1)
                    ring_forward(d, 1, -1)
                else:
                    ring_forward(d, 0, -1)
                    ring_forward(d, 1, -1)

    for c in range(n_chunk + 2):
        if c < n_chunk:
            x_start(c)
        if c == 0:
            side_tables()
        if 0 <= c - 1 < n_chunk:
            x_forward(c - 1)
        if 0 <= c - 2 < n_chunk:
            x_finish(c - 2)
            if c == 2:
                core_copy.wait_recv()
            grams(c - 2)
            ring(c - 2)
    totals = [gram[slots.index((0, z))] + arrived(0, z, 1) + arrived(0, z, -1) for z in range(2)]
    kept, passed = slots.index((0, 0)), slots.index((0, 1))
    swap = z_low == 0
    gram[kept] = jnp.where(swap, totals[0], totals[1])
    gram[passed] = jnp.where(swap, totals[1], totals[0])
    z_sum = remote(gram.at[passed], got_z, zx_sem.at[0], zx_sem.at[1], z_partner)
    send(z_sum)
    z_sum.wait_recv()
    total = gram[kept] + got_z[...]

    real, imag = total[:n_src], total[n_src:]
    upper = lax.rem(iota((n_src, LANES), 0), 8) < SHOTS
    first = jnp.where(upper, real, pltpu.roll(imag, SHOTS, 0))
    second = jnp.where(upper, pltpu.roll(real, n_src - SHOTS, 0), imag)
    for a in range(n_grp // 2):
        tiles[2 * a] = first[8 * a : 8 * a + 8]
        tiles[2 * a + 1] = second[8 * a : 8 * a + 8]

    def tile_copy(d):
        target = lax.rem(grp + d, n_grp)
        return pltpu.make_async_remote_copy(
            src_ref=tiles.at[target], dst_ref=got_tiles.at[grp], send_sem=aa_send.at[d], recv_sem=aa_recv.at[d],
            device_id=device(chip, core, target), device_id_type=MESH,
        )

    for d in range(1, n_grp):
        sends.append(tile_copy(d))
        sends[-1].start()
    got_tiles[grp] = tiles[grp]
    for d in range(1, n_grp):
        tile_copy(d).wait_recv()

    field = jnp.concatenate([got_tiles[g] for g in range(n_grp)], axis=1)
    field_high = field.astype(BF16).astype(F32)
    field_low = field - field_high
    mask = x_mask[...]

    def placed(part):
        return jnp.concatenate(
            [jnp.broadcast_to(part[i : i + 1], (grid_x, receivers)).astype(BF16) * mask for i in range(2 * SHOTS)], axis=0
        )

    section = dot_lanes(placed(field_high), y_phase[...])
    section = section[:, :LANES] + section[:, LANES:] + dot_lanes(placed(field_low), y_phase[0:LANES])
    half = SHOTS * grid_x
    lower = iota((half, LANES), 1) < GY
    plus_minus = jnp.where(lower, 1.0, -1.0)
    section = plus_minus * section[:half] + pltpu.roll(section[half:], GY, 1)
    turned_section = plus_minus * pltpu.roll(section, GY, 1)
    stacked = jnp.concatenate([section, turned_section], axis=0)
    stacked_high, stacked_low = split(stacked)
    both = dot(forward_x[0], jnp.concatenate([stacked_high, stacked_low], axis=1))
    spec = both[:, :LANES] + both[:, LANES:] + dot(forward_x[1], stacked_high)
    spec_turned = pltpu.roll(spec, GY, 1)
    spec3, spec3_turned = spec.reshape(SHOTS, grid_x, LANES), spec_turned.reshape(SHOTS, grid_x, LANES)
    for p in range(2):
        shifted = [
            (spec3 * shift[k, 0][None] + spec3_turned * shift[k, 1][None]).reshape(half, LANES) for k in (2 * p, 2 * p + 1)
        ]
        back = dot3(jnp.concatenate(shifted, axis=1), inverse_y[0], inverse_y[1])
        back = jnp.concatenate([back[:, :LANES], back[:, LANES:]], axis=0)
        back_high, back_low = split(back)
        both = dot(inverse_x[0], jnp.concatenate([back_high, back_low], axis=1))
        picture = both[:, :LANES] + both[:, LANES:] + dot(inverse_x[1], back_high)
        energies = jnp.sum((picture * picture).reshape(SHOTS, grid_x, LANES), axis=0)
        for g in range(n_grp):
            energy[g, 2 * p : 2 * p + 2] = energies[2 * g : 2 * g + 2]

    def energy_copy(d):
        target = lax.rem(grp + d, n_grp)
        return pltpu.make_async_remote_copy(
            src_ref=energy.at[target], dst_ref=got_energy.at[d], send_sem=en_send.at[d], recv_sem=en_recv.at[d],
            device_id=device(chip, core, target), device_id_type=MESH,
        )

    for d in range(1, n_grp):
        sends.append(energy_copy(d))
        sends[-1].start()
    image = energy[grp]
    for d in range(1, n_grp):
        energy_copy(d).wait_recv()
        image += got_energy[d]
    n_windows = windows * n_win
    scale = 1.0 / (n_src * grid_x * GY * n_windows * n_windows)
    for p in range(2):
        one, two = image[2 * p : 2 * p + 1] * scale, image[2 * p + 1 : 2 * p + 2] * scale
        low = iota((1, LANES), 1) < GY
        out[2 * p : 2 * p + 1] = jnp.where(low, one, pltpu.roll(two, GY, 1))
        out[2 * p + 1 : 2 * p + 2] = jnp.where(low, pltpu.roll(one, GY, 1), two)

    for copy in sends:
        copy.wait_send()


def body(n_grp, n_win, spectra, freq_bins, slowness, positions):
    freqs, windows, _, block = spectra.shape
    grid_x = 2 * n_grp
    n_freq = n_win // 2
    n_chunk = n_freq * SHOTS // 16
    n_z = n_grp // N_X
    rows = 2 * windows
    n_src = SHOTS * n_grp
    receivers = n_grp * block
    hbm = pl.BlockSpec(memory_space=pltpu.HBM)
    dma = pltpu.SemaphoreType.DMA
    consts = tables(grid_x)
    image = pl.pallas_call(
        functools.partial(kernel, n_grp, n_win, windows),
        out_shape=jax.ShapeDtypeStruct((4, block), F32),
        in_specs=[hbm] * (4 + len(consts)),
        out_specs=pl.BlockSpec(memory_space=pltpu.VMEM),
        scratch_shapes=[
            pltpu.VMEM((1, receivers), jnp.int32),
            pltpu.SMEM((n_win,), jnp.int32),
            pltpu.SMEM((4,), F32),
            *(pltpu.VMEM(c.shape, c.dtype) for c in consts),
            pltpu.VMEM((n_freq, 2, rows, block), BF16),
            pltpu.VMEM((n_freq, rows, block), BF16),
            pltpu.VMEM((n_chunk, n_grp, 2, 16, rows), BF16),
            pltpu.VMEM((n_chunk, 16, rows), BF16),
            pltpu.VMEM((n_freq, 2 * n_src, block), F32),
            pltpu.VMEM((n_freq // 2, 2 * n_src, block), F32),
            pltpu.VMEM((n_freq // 2, 2 * n_src, block), F32),
            pltpu.VMEM((2 * n_src, block), F32),
            pltpu.VMEM((n_grp, 2 * SHOTS, block), F32),
            pltpu.VMEM((n_grp, 2 * SHOTS, block), F32),
            pltpu.VMEM((n_grp, SHOTS, block), F32),
            pltpu.VMEM((n_grp, SHOTS, block), F32),
            pltpu.VMEM((2 * LANES, receivers), BF16),
            pltpu.VMEM((grid_x, receivers), BF16),
            pltpu.VMEM((4, 2, grid_x, LANES), F32),
            dma((5 + len(consts),)), dma((4,)),
            dma((n_chunk, n_z)), dma((n_chunk, n_z)), dma((n_chunk, 4)), dma((n_chunk, 4)),
            dma((2, n_freq // 2)), dma((2, n_freq // 2)), dma((2,)),
            dma((n_grp,)), dma((n_grp,)), dma((n_grp,)), dma((n_grp,)),
        ],
        compiler_params=pltpu.CompilerParams(
            collective_id=0, has_side_effects=True, vmem_limit_bytes=63 * 1024 * 1024
        ),
    )(
        spectra.reshape(n_freq, 2, rows, block),
        positions.reshape(1, receivers),
        freq_bins,
        slowness,
        *(jnp.asarray(c) for c in consts),
    )
    return image[None]


def solution(mesh):
    return jax.shard_map(
        functools.partial(body, mesh.shape["grp"], mesh.shape["win"]),
        mesh=mesh,
        in_specs=(P(None, "win", None, "grp"), P(), P(), P()),
        out_specs=P("win", None, "grp"),
        check_vma=False,
    )
```

time: 87.3 us -> 66.6 us (0.76)
  Pallas kernels: 78.4 us -> 64.3 us
  local copies, waits for them, and re-layouts: 8.49 us -> 1.26 us
    pallas_call x1, Pallas kernels: 78.4 us -> 64.3 us  [body(): pl.pallas_call(functools.partial(kernel, n_grp, n_win, windows), out_shap...]
    unnamed x19 -> x1, local copies, waits for them, and re-layouts: 8.49 us -> 1.26 us
where the time goes in v2:
time: 66.6 us; the launch traced here: 65.5 us
  Pallas kernels  64.3 us (97%)
  local copies, waits for them, and re-layouts  1.26 us (2%)
    pallas_call x1, Pallas kernels, body(): pl.pallas_call(functools.partial(kernel, n_grp, n_win, windows), out_shap...  64.3 us

profile of v2, /device:TPU:6, one launch (start us, length us, event | category | flops | bytes accessed | tf_op | source)
XLA Modules:
  0.0 65.5 jit_solution(18362527784726046878)
XLA Ops:
  0.0 64.3 %shard_map.91 = f32[4,128]{1,0:T(4,128)} custom-call(bf16[16,2,256,128]{3,2,1,0:T(8,128)(2,1)} %bitcast.3, s32[1,2048]{1,0:T(1,128)} %bitcast.4, s32[32]{0:T(128)} %freq_hbm.1, f32[4]{0:T(128)} %slowness_hbm.1, bf16[2,128,64]{2,1,0:T(8,128)(2,1)} %constant.10.clone.rows_hbm, bf16[2,128,256]{2,1,0:T(8,128)(2,1)} %constant.11.clone.forward_hbm, ...), custom_call_target="tpu_custom_call" | custom-call | tf_op jit(solution)/shard_map/pallas_call | solution.py:438
  64.3 1.3 %copy.11 = f32[1,4,128]{2,1,0:T(4,128)} copy(f32[1,4,128]{2,1,0:T(4,128)} %bitcast.5) | data formatting | bytes 4096

commit v3 on v2

--- a/solution.py
+++ b/solution.py
@@ -35,6 +35,23 @@
     width = b_high.shape[1]
     both = dot(high, jnp.concatenate([b_high, b_low], axis=1))
     return both[:, :width] + both[:, width:] + dot(low, b_high)
+
+
+CODE_TOP = 32767.0
+EXTRA = 16
+
+
+def coded(block):
+    top = jnp.max(jnp.abs(block), axis=0, keepdims=True)
+    exponent = jnp.ceil(jnp.log2(jnp.maximum(top, 1e-30)))
+    values = jnp.clip(jnp.round(block * (CODE_TOP * jnp.exp2(-exponent))), -CODE_TOP, CODE_TOP)
+    return jnp.concatenate([values, jnp.broadcast_to(exponent, (EXTRA, LANES))], axis=0).astype(jnp.int32).astype(jnp.int16)
+
+
+def decoded(code):
+    values = code.astype(jnp.int32).astype(F32)
+    rows = code.shape[0] - EXTRA
+    return values[:rows] * (jnp.exp2(values[rows : rows + 1]) * (1.0 / CODE_TOP))
 
 
 def np_split(table):
@@ -89,9 +106,9 @@
     spectra, positions_hbm, freq_hbm, slowness_hbm, rows_hbm, forward_hbm, inverse_x_hbm, inverse_y_hbm, squares_hbm,
     out,
     positions, freq_bins, slowness, rows_y, forward_x, inverse_x, inverse_y, squares,
-    u, v, picked, theirs, gram, got_plus, got_minus, got_z, tiles, got_tiles, energy, got_energy,
+    u, v, picked, theirs, own_gram, blocks, got_blocks, tiles, got_tiles, energy, got_energy,
     y_phase, x_mask, shift,
-    local_sem, core_sem, z_send, z_recv, x_send, x_recv, rs_send, rs_recv, zx_sem, aa_send, aa_recv, en_send, en_recv,
+    local_sem, core_sem, z_send, z_recv, x_send, x_recv, rs_send, rs_recv, aa_send, aa_recv, en_send, en_recv,
 ):
     n_freq = n_win // 2
     n_y = n_freq // 2
@@ -129,11 +146,21 @@
         copy.start()
         sends.append(copy)
 
+    def hops(offset):
+        return min(offset[0], N_X - offset[0]) + 2 * min(offset[1], n_z - offset[1])
+
+    offsets = sorted(((a, b) for a in range(N_X) for b in range(n_z)), key=hops, reverse=True)
+    away = offsets[:-1]
+    far_z = sorted(range(1, n_z), key=lambda d: -min(d, n_z - d))
+    far_x = sorted(range(1, N_X), key=lambda d: -min(d, N_X - d))
+
+    def to(offset):
+        return at_x(offset[0]) * n_z + at_zh(offset[1])
+
     partner = device(chip, other, grp)
-    z_partner = device(y * 2 + 1 - z_low, core, grp)
     barrier = pltpu.get_barrier_semaphore()
-    greeted = [partner, z_partner, device(at_y(1) * 2 + z_low, core, grp), device(at_y(-1) * 2 + z_low, core, grp)]
-    greeted += [device(chip, core, lax.rem(grp + d, n_grp)) for d in range(1, n_grp)]
+    greeted = [device(chip, core, to(o)) for o in away]
+    greeted += [device(lax.rem(chip + d, n_freq), core, grp) for d in range(1, n_freq)] + [partner]
     for target in greeted:
         pl.semaphore_signal(barrier, inc=1, device_id=target, device_id_type=MESH)
 
@@ -157,7 +184,8 @@
     for load in loads:
         load.start()
 
-    ahead = [n_y // 2] + [d for k in range(n_y // 2 - 1, 0, -1) for d in (k, -k)] + [0]
+    ahead = [4, 3, -3, 2, 1, -2, -1, 0]
+    assert n_y == len(ahead)
     slots = [(d, z) for d in ahead for z in range(2)]
     chunk = 16 // SHOTS
     n_chunk = n_freq // chunk
@@ -176,49 +204,47 @@
         for_partner += dot_lanes(pick, v[freq_of(slot)])
     own, for_partner = own.astype(BF16), for_partner.astype(BF16)
     for c in range(n_chunk):
-        picked[c, grp, core] = own[16 * c : 16 * c + 16]
+        picked[c, x, zh, core] = own[16 * c : 16 * c + 16]
         theirs[c] = for_partner[16 * c : 16 * c + 16]
 
     pl.semaphore_wait(barrier, len(greeted))
 
-    pick_copy = remote(theirs, picked.at[:, grp, core], core_sem.at[0], core_sem.at[1], partner)
+    pick_copy = remote(theirs, picked.at[:, x, zh, core], core_sem.at[0], core_sem.at[1], partner)
     send(pick_copy)
     core_copy = remote(v, u.at[:, core], core_sem.at[2], core_sem.at[3], partner)
     send(core_copy)
     pick_copy.wait_recv()
 
-    def z_copy(c, d, holder):
-        return remote(
-            picked.at[c, holder], picked.at[c, holder], z_send.at[c, d], z_recv.at[c, d],
-            device(chip, core, x * n_z + at_zh(d)),
-        )
-
-    def x_copy(c, holder_x, first, count, step, kind):
-        part = pl.ds(holder_x * n_z + first, count)
-        sem = 2 * kind + (0 if step > 0 else 1)
-        return remote(
-            picked.at[c, part], picked.at[c, part], x_send.at[c, sem], x_recv.at[c, sem],
-            device(chip, core, at_x(step) * n_z + zh),
-        )
-
-    for c in range(n_chunk):
-        for d in range(1, n_z):
-            send(z_copy(c, d, grp))
+    mixed = n_chunk - 2
+
+    def z_copy(c, d, from_zh):
+        part = picked.at[c, :, from_zh] if c == mixed else picked.at[c, x, from_zh]
+        return remote(part, part, z_send.at[c, d], z_recv.at[c, d], device(chip, core, x * n_z + at_zh(d)))
+
+    def x_copy(c, d, from_x):
+        part = picked.at[c, from_x, zh] if c == mixed else picked.at[c, from_x]
+        return remote(part, part, x_send.at[c, d], x_recv.at[c, d], device(chip, core, at_x(d) * n_z + zh))
+
+    def z_start(c):
+        for d in far_z:
+            send(z_copy(c, d, zh))
 
     def x_start(c):
-        for d in range(1, n_z):
-            z_copy(c, d, x * n_z + at_zh(-d)).wait_recv()
-        for step in (1, -1):
-            send(x_copy(c, x, 0, n_z, step, 0))
-
-    def x_forward(c):
-        for step in (1, -1):
-            x_copy(c, at_x(-step), 0, n_z, step, 0).wait_recv()
-            send(x_copy(c, at_x(-step), 0 if step > 0 else n_z // 2, n_z // 2, step, 1))
-
-    def x_finish(c):
-        for step in (1, -1):
-            x_copy(c, at_x(-2 * step), 0 if step > 0 else n_z // 2, n_z // 2, step, 1).wait_recv()
+        for d in far_x:
+            send(x_copy(c, d, x))
+
+    def z_wait(c):
+        for d in reversed(far_z):
+            z_copy(c, d, at_zh(-d)).wait_recv()
+
+    def x_wait(c):
+        for d in reversed(far_x):
+            x_copy(c, d, at_x(-d)).wait_recv()
+
+    legs = [(x_start, x_wait, z_start, z_wait) if c == mixed else (z_start, z_wait, x_start, x_wait) for c in range(n_chunk)]
+    early = [0, mixed] + [c for c in range(1, n_chunk) if c != mixed] if mixed else list(range(n_chunk))
+    for c in early:
+        legs[c][0](c)
 
     def side_tables():
         for load in loads[2:]:
@@ -256,8 +282,9 @@
     def grams(c):
         sources = []
         for half in range(2):
-            plain = dot(reorder, picked[c, :, half].reshape(height, rows)).astype(BF16)
+            plain = dot(reorder, picked[c, :, :, half].reshape(height, rows)).astype(BF16)
             sources.append((plain, dot(plain, turn).astype(BF16)))
+        first_here = None
         for i in range(chunk):
             slot = chunk * c + i
             q = freq_of(slot)
@@ -266,100 +293,73 @@
                 left = jnp.concatenate([plain[n_src * i : n_src * (i + 1)], turned[n_src * i : n_src * (i + 1)]], axis=0)
                 term = dot(left, u[q, half])
                 result = term if result is None else result + term
-            gram[slot] = result
-
-    def ring_copy(d, z, step):
-        slot = slots.index((abs(d) if abs(d) == n_y // 2 else d, z))
-        index = (abs(d) - 1) * 2 + z
-        got = got_plus if step > 0 else got_minus
-        lane_ = 0 if step > 0 else 1
+            d, z = slots[slot]
+            if abs(d) == 2:
+                for passed in ((2 * d, 3 * d // 2) if (d > 0) == (z == 0) else (3 * d // 2,)):
+                    result += block_arrived(slots.index((abs(passed) if passed == -4 else passed, z)))
+            if d:
+                block_send(slot, result)
+            elif z == 0:
+                first_here = result
+            else:
+                here = z_low == 0
+                own_gram[...] = jnp.where(here, first_here, result)
+                block_send(slot, jnp.where(here, result, first_here))
+
+    def block_copy(slot):
+        d, z = slots[slot]
+        if abs(d) > 2:
+            step = (2 if z == 0 else -2) if d == 4 else d // 3
+            target, index = at_y(step) * 2 + z_low, slot
+        else:
+            target = at_y(d) * 2 + (z if d else 1 - z_low)
+            index = slot - slot % 2 + z_low
         return remote(
-            gram.at[slot], got.at[index], rs_send.at[lane_, index], rs_recv.at[lane_, index],
-            device(at_y(step) * 2 + z_low, core, grp),
-        )
-
-    def ring_start(d, z, step):
-        send(ring_copy(d, z, step))
-
-    def arrived(d, z, step):
-        ring_copy(d + step, z, step).wait_recv()
-        got = got_plus if step > 0 else got_minus
-        return got[(abs(d + step) - 1) * 2 + z]
-
-    def ring_forward(d, z, step):
-        slot = slots.index((d, z))
-        gram[slot] = gram[slot] + arrived(d, z, step)
-        ring_start(d, z, step)
-
-    far = n_y // 2
-
-    def ring(c):
-        for place in (2 * c - 1, 2 * c):
-            if place < 0:
-                continue
-            d = ahead[place]
-            if d == far:
-                ring_start(far, 0, 1)
-                ring_start(-far, 1, -1)
-                ring_start(far - 1, 1, 1)
-            elif d > 0:
-                if d == far - 1:
-                    ring_forward(d, 0, 1)
-                else:
-                    ring_forward(d, 1, 1)
-                    ring_forward(d, 0, 1)
-            elif d < 0:
-                if d == 1 - far:
-                    ring_start(d, 0, -1)
-                    ring_forward(d, 1, -1)
-                else:
-                    ring_forward(d, 0, -1)
-                    ring_forward(d, 1, -1)
-
-    for c in range(n_chunk + 2):
-        if c < n_chunk:
-            x_start(c)
-        if c == 0:
-            side_tables()
-        if 0 <= c - 1 < n_chunk:
-            x_forward(c - 1)
-        if 0 <= c - 2 < n_chunk:
-            x_finish(c - 2)
-            if c == 2:
-                core_copy.wait_recv()
-            grams(c - 2)
-            ring(c - 2)
-    totals = [gram[slots.index((0, z))] + arrived(0, z, 1) + arrived(0, z, -1) for z in range(2)]
-    kept, passed = slots.index((0, 0)), slots.index((0, 1))
-    swap = z_low == 0
-    gram[kept] = jnp.where(swap, totals[0], totals[1])
-    gram[passed] = jnp.where(swap, totals[1], totals[0])
-    z_sum = remote(gram.at[passed], got_z, zx_sem.at[0], zx_sem.at[1], z_partner)
-    send(z_sum)
-    z_sum.wait_recv()
-    total = gram[kept] + got_z[...]
-
+            blocks.at[slot], got_blocks.at[index], rs_send.at[slot], rs_recv.at[index], device(target, core, grp)
+        )
+
+    def block_send(slot, value):
+        blocks[slot] = coded(value)
+        send(block_copy(slot))
+
+    def block_arrived(index):
+        remote(
+            blocks.at[0], got_blocks.at[index], rs_send.at[0], rs_recv.at[index], device(at_y(1) * 2 + z_low, core, grp)
+        ).wait_recv()
+        return decoded(got_blocks[index])
+
+    side_tables()
+    for c in early:
+        legs[c][1](c)
+        legs[c][2](c)
+    core_copy.wait_recv()
+    for c in range(n_chunk):
+        legs[c][3](c)
+        grams(c)
+    total = own_gram[...]
+    for index in range(6, n_freq - 2):
+        total += block_arrived(index)
+    total += block_arrived(n_freq - 1 - z_low)
+
+    upper = lax.rem(iota((n_src, LANES), 0), 8) < SHOTS
     real, imag = total[:n_src], total[n_src:]
-    upper = lax.rem(iota((n_src, LANES), 0), 8) < SHOTS
     first = jnp.where(upper, real, pltpu.roll(imag, SHOTS, 0))
     second = jnp.where(upper, pltpu.roll(real, n_src - SHOTS, 0), imag)
     for a in range(n_grp // 2):
         tiles[2 * a] = first[8 * a : 8 * a + 8]
         tiles[2 * a + 1] = second[8 * a : 8 * a + 8]
 
-    def tile_copy(d):
-        target = lax.rem(grp + d, n_grp)
-        return pltpu.make_async_remote_copy(
-            src_ref=tiles.at[target], dst_ref=got_tiles.at[grp], send_sem=aa_send.at[d], recv_sem=aa_recv.at[d],
-            device_id=device(chip, core, target), device_id_type=MESH,
-        )
-
-    for d in range(1, n_grp):
-        sends.append(tile_copy(d))
-        sends[-1].start()
+    def tile_copy(i):
+        target = to(away[i])
+        return remote(
+            tiles.at[target], got_tiles.at[grp], aa_send.at[i], aa_recv.at[i], device(chip, core, target)
+        )
+
+    for i in range(n_grp - 1):
+        send(tile_copy(i))
     got_tiles[grp] = tiles[grp]
-    for d in range(1, n_grp):
-        tile_copy(d).wait_recv()
+    for i in reversed(range(n_grp - 1)):
+        tile_copy(i).wait_recv()
 
     field = jnp.concatenate([got_tiles[g] for g in range(n_grp)], axis=1)
     field_high = field.astype(BF16).astype(F32)
@@ -397,20 +397,18 @@
         for g in range(n_grp):
             energy[g, 2 * p : 2 * p + 2] = energies[2 * g : 2 * g + 2]
 
-    def energy_copy(d):
-        target = lax.rem(grp + d, n_grp)
-        return pltpu.make_async_remote_copy(
-            src_ref=energy.at[target], dst_ref=got_energy.at[d], send_sem=en_send.at[d], recv_sem=en_recv.at[d],
-            device_id=device(chip, core, target), device_id_type=MESH,
-        )
-
-    for d in range(1, n_grp):
-        sends.append(energy_copy(d))
-        sends[-1].start()
+    def energy_copy(i):
+        target = to(away[i])
+        return remote(
+            energy.at[target], got_energy.at[i], en_send.at[i], en_recv.at[i], device(chip, core, target)
+        )
+
+    for i in range(n_grp - 1):
+        send(energy_copy(i))
     image = energy[grp]
-    for d in range(1, n_grp):
-        energy_copy(d).wait_recv()
-        image += got_energy[d]
+    for i in reversed(range(n_grp - 1)):
+        energy_copy(i).wait_recv()
+        image += got_energy[i]
     n_windows = windows * n_win
     scale = 1.0 / (n_src * grid_x * GY * n_windows * n_windows)
     for p in range(2):
@@ -447,12 +445,11 @@
             *(pltpu.VMEM(c.shape, c.dtype) for c in consts),
             pltpu.VMEM((n_freq, 2, rows, block), BF16),
             pltpu.VMEM((n_freq, rows, block), BF16),
-            pltpu.VMEM((n_chunk, n_grp, 2, 16, rows), BF16),
+            pltpu.VMEM((n_chunk, N_X, n_z, 2, 16, rows), BF16),
             pltpu.VMEM((n_chunk, 16, rows), BF16),
-            pltpu.VMEM((n_freq, 2 * n_src, block), F32),
-            pltpu.VMEM((n_freq // 2, 2 * n_src, block), F32),
-            pltpu.VMEM((n_freq // 2, 2 * n_src, block), F32),
             pltpu.VMEM((2 * n_src, block), F32),
+            pltpu.VMEM((n_freq, 2 * n_src + EXTRA, block), jnp.int16),
+            pltpu.VMEM((n_freq, 2 * n_src + EXTRA, block), jnp.int16),
             pltpu.VMEM((n_grp, 2 * SHOTS, block), F32),
             pltpu.VMEM((n_grp, 2 * SHOTS, block), F32),
             pltpu.VMEM((n_grp, SHOTS, block), F32),
@@ -461,8 +458,8 @@
             pltpu.VMEM((grid_x, receivers), BF16),
             pltpu.VMEM((4, 2, grid_x, LANES), F32),
             dma((5 + len(consts),)), dma((4,)),
-            dma((n_chunk, n_z)), dma((n_chunk, n_z)), dma((n_chunk, 4)), dma((n_chunk, 4)),
-            dma((2, n_freq // 2)), dma((2, n_freq // 2)), dma((2,)),
+            dma((n_chunk, n_z)), dma((n_chunk, n_z)), dma((n_chunk, N_X)), dma((n_chunk, N_X)),
+            dma((n_freq,)), dma((n_freq,)),
             dma((n_grp,)), dma((n_grp,)), dma((n_grp,)), dma((n_grp,)),
         ],
         compiler_params=pltpu.CompilerParams(

time: 66.6 us -> 57.4 us (0.86)
  Pallas kernels: 64.3 us -> 55.3 us
    pallas_call x1, Pallas kernels: 64.3 us -> 55.3 us  [body(): pl.pallas_call(functools.partial(kernel, n_grp, n_win, windows), out_shap...]
where the time goes in v3:
time: 57.4 us; the launch traced here: 56.6 us
  Pallas kernels  55.3 us (96%)
  local copies, waits for them, and re-layouts  1.26 us (2%)
    pallas_call x1, Pallas kernels, body(): pl.pallas_call(functools.partial(kernel, n_grp, n_win, windows), out_shap...  55.3 us
    unnamed x1, local copies, waits for them, and re-layouts  1.26 us

profile of v3, /device:TPU:6, one launch (start us, length us, event | category | flops | bytes accessed | tf_op | source)
XLA Modules:
  0.0 56.6 jit_solution(3870853981058890111)
XLA Ops:
  0.0 55.3 %shard_map.91 = f32[4,128]{1,0:T(4,128)} custom-call(bf16[16,2,256,128]{3,2,1,0:T(8,128)(2,1)} %bitcast.3, s32[1,2048]{1,0:T(1,128)} %bitcast.4, s32[32]{0:T(128)} %freq_hbm.1, f32[4]{0:T(128)} %slowness_hbm.1, bf16[2,128,64]{2,1,0:T(8,128)(2,1)} %constant.10.clone.rows_hbm, bf16[2,128,256]{2,1,0:T(8,128)(2,1)} %constant.11.clone.forward_hbm, ...), custom_call_target="tpu_custom_call" | custom-call | tf_op jit(solution)/shard_map/pallas_call | solution.py:436
  55.3 1.3 %copy.11 = f32[1,4,128]{2,1,0:T(4,128)} copy(f32[1,4,128]{2,1,0:T(4,128)} %bitcast.5) | data formatting | bytes 4096

commit v4 on v3

--- a/solution.py
+++ b/solution.py
@@ -108,7 +108,7 @@
     positions, freq_bins, slowness, rows_y, forward_x, inverse_x, inverse_y, squares,
     u, v, picked, theirs, own_gram, blocks, got_blocks, tiles, got_tiles, energy, got_energy,
     y_phase, x_mask, shift,
-    local_sem, core_sem, z_send, z_recv, x_send, x_recv, rs_send, rs_recv, aa_send, aa_recv, en_send, en_recv,
+    local_sem, core_sem, pick_send, pick_recv, first_send, first_recv, second_send, second_recv, rs_send, rs_recv, tile_sem, energy_sem,
 ):
     n_freq = n_win // 2
     n_y = n_freq // 2
@@ -140,11 +140,21 @@
             src_ref=src, dst_ref=dst, send_sem=send_sem, recv_sem=recv_sem, device_id=target, device_id_type=MESH
         )
 
-    sends = []
+    ends = []
 
     def send(copy):
         copy.start()
-        sends.append(copy)
+        ends.append(copy)
+
+    def send_all(copies, whole):
+        for copy in copies:
+            copy.start()
+        ends.append(whole)
+
+    def drain():
+        for copy in ends:
+            copy.wait_send()
+        ends.clear()
 
     def hops(offset):
         return min(offset[0], N_X - offset[0]) + 2 * min(offset[1], n_z - offset[1])
@@ -158,12 +168,6 @@
         return at_x(offset[0]) * n_z + at_zh(offset[1])
 
     partner = device(chip, other, grp)
-    barrier = pltpu.get_barrier_semaphore()
-    greeted = [device(chip, core, to(o)) for o in away]
-    greeted += [device(lax.rem(chip + d, n_freq), core, grp) for d in range(1, n_freq)] + [partner]
-    for target in greeted:
-        pl.semaphore_signal(barrier, inc=1, device_id=target, device_id_type=MESH)
-
     loads = [
         pltpu.make_async_copy(source, target, local_sem.at[i])
         for i, (source, target) in enumerate(
@@ -184,6 +188,14 @@
     for load in loads:
         load.start()
 
+    barrier = pltpu.get_barrier_semaphore()
+    greeted = [device(chip, core, to(o)) for o in away]
+    greeted += [device(at_y(d) * 2 + z, core, grp) for d in (2, -2, 1, -1) for z in range(2)]
+    greeted += [device(y * 2 + 1 - z_low, core, grp), partner]
+    greeted += [device(chip, other, to(o)) for o in away if 0 in o]
+    for target in greeted:
+        pl.semaphore_signal(barrier, inc=1, device_id=target, device_id_type=MESH)
+
     ahead = [4, 3, -3, 2, 1, -2, -1, 0]
     assert n_y == len(ahead)
     slots = [(d, z) for d in ahead for z in range(2)]
@@ -204,47 +216,62 @@
         for_partner += dot_lanes(pick, v[freq_of(slot)])
     own, for_partner = own.astype(BF16), for_partner.astype(BF16)
     for c in range(n_chunk):
-        picked[c, x, zh, core] = own[16 * c : 16 * c + 16]
+        picked[c, x, 0, core] = own[16 * c : 16 * c + 16]
         theirs[c] = for_partner[16 * c : 16 * c + 16]
 
     pl.semaphore_wait(barrier, len(greeted))
 
-    pick_copy = remote(theirs, picked.at[:, x, zh, core], core_sem.at[0], core_sem.at[1], partner)
-    send(pick_copy)
-    core_copy = remote(v, u.at[:, core], core_sem.at[2], core_sem.at[3], partner)
+    mixed = n_chunk - 2
+
+    def first_copy(c, axis, d, to_core):
+        peer = to((d, 0) if axis == 0 else (0, d))
+        source = picked.at[c, x, 0, core] if to_core == 0 else theirs.at[c]
+        return remote(
+            source, picked.at[c, x, (n_z - d) % n_z if axis else 0, core], first_send.at[c, axis], first_recv.at[c, axis],
+            device(chip, other if to_core else core, peer),
+        )
+
+    def first_whole(c, axis):
+        part = picked.at[c, x, 1:] if axis else picked.at[c, 1:, 0]
+        return remote(part, part, first_send.at[c, axis], first_recv.at[c, axis], partner)
+
+    def first_start(c, axis):
+        send_all(
+            [first_copy(c, axis, d, to_core) for d in (far_z if axis else far_x) for to_core in range(2)],
+            first_whole(c, axis),
+        )
+
+    def second_copy(c, d):
+        if c == mixed:
+            source, target, offset = picked.at[c, :, 0], picked.at[c, :, n_z - d], (0, d)
+        else:
+            source, target, offset = picked.at[c, x, 1:], picked.at[c, x, 1:], (d, 0)
+        return remote(source, target, second_send.at[c], second_recv.at[c], device(chip, core, to(offset)))
+
+    def second_whole(c):
+        part = picked.at[c, :, 1:] if c == mixed else picked.at[c, 1:, 1:]
+        return remote(part, part, second_send.at[c], second_recv.at[c], partner)
+
+    def second_start(c):
+        send_all([second_copy(c, d) for d in (far_z if c == mixed else far_x)], second_whole(c))
+
+    def second_wait(c):
+        second_whole(c).wait_recv()
+        if c != mixed:
+            first_whole(c, 0).wait_recv()
+
+    pick_copies = [
+        remote(theirs.at[c], picked.at[c, x, 0, core], pick_send.at[c], pick_recv.at[c], partner) for c in range(n_chunk)
+    ]
+    core_copy = remote(v, u.at[:, core], core_sem.at[0], core_sem.at[1], partner)
+    early = [0, mixed] + [c for c in range(1, n_chunk) if c != mixed]
+    for c in early:
+        send(pick_copies[c])
+        first_start(c, 0 if c == mixed else 1)
+    for c in range(n_chunk):
+        if c != mixed:
+            first_start(c, 0)
     send(core_copy)
-    pick_copy.wait_recv()
-
-    mixed = n_chunk - 2
-
-    def z_copy(c, d, from_zh):
-        part = picked.at[c, :, from_zh] if c == mixed else picked.at[c, x, from_zh]
-        return remote(part, part, z_send.at[c, d], z_recv.at[c, d], device(chip, core, x * n_z + at_zh(d)))
-
-    def x_copy(c, d, from_x):
-        part = picked.at[c, from_x, zh] if c == mixed else picked.at[c, from_x]
-        return remote(part, part, x_send.at[c, d], x_recv.at[c, d], device(chip, core, at_x(d) * n_z + zh))
-
-    def z_start(c):
-        for d in far_z:
-            send(z_copy(c, d, zh))
-
-    def x_start(c):
-        for d in far_x:
-            send(x_copy(c, d, x))
-
-    def z_wait(c):
-        for d in reversed(far_z):
-            z_copy(c, d, at_zh(-d)).wait_recv()
-
-    def x_wait(c):
-        for d in reversed(far_x):
-            x_copy(c, d, at_x(-d)).wait_recv()
-
-    legs = [(x_start, x_wait, z_start, z_wait) if c == mixed else (z_start, z_wait, x_start, x_wait) for c in range(n_chunk)]
-    early = [0, mixed] + [c for c in range(1, n_chunk) if c != mixed] if mixed else list(range(n_chunk))
-    for c in early:
-        legs[c][0](c)
 
     def side_tables():
         for load in loads[2:]:
@@ -274,7 +301,9 @@
     height = 16 * n_grp
     row, lane = iota((height, height), 0), iota((height, height), 1)
     slot_of, src_of = lax.div(row, n_src), lax.rem(row, n_src)
-    reorder = one_hot(lane == lax.div(src_of, SHOTS) * 16 + slot_of * SHOTS + lax.rem(src_of, SHOTS))
+    origin = lax.div(src_of, SHOTS)
+    held = lax.div(origin, n_z) * n_z + lax.rem(lax.rem(origin, n_z) + n_z - zh, n_z)
+    reorder = one_hot(lane == held * 16 + slot_of * SHOTS + lax.rem(src_of, SHOTS))
     row, lane = iota((rows, rows), 0), iota((rows, rows), 1)
     even = lax.rem(row, 2) == 0
     turn = jnp.where(~even & (lane == row - 1), -1.0, jnp.where(even & (lane == row + 1), 1.0, 0.0)).astype(BF16)
@@ -330,11 +359,12 @@
 
     side_tables()
     for c in early:
-        legs[c][1](c)
-        legs[c][2](c)
+        pick_copies[c].wait_recv()
+        first_whole(c, 0 if c == mixed else 1).wait_recv()
+        second_start(c)
     core_copy.wait_recv()
     for c in range(n_chunk):
-        legs[c][3](c)
+        second_wait(c)
         grams(c)
     total = own_gram[...]
     for index in range(6, n_freq - 2):
@@ -349,17 +379,20 @@
         tiles[2 * a] = first[8 * a : 8 * a + 8]
         tiles[2 * a + 1] = second[8 * a : 8 * a + 8]
 
-    def tile_copy(i):
-        target = to(away[i])
+    def tile_copy(offset):
+        target = to(offset)
         return remote(
-            tiles.at[target], got_tiles.at[grp], aa_send.at[i], aa_recv.at[i], device(chip, core, target)
-        )
-
-    for i in range(n_grp - 1):
-        send(tile_copy(i))
+            tiles.at[target], got_tiles.at[grp], tile_sem.at[0], tile_sem.at[1], device(chip, core, target)
+        )
+
+    tiles_whole = remote(tiles.at[1:], got_tiles.at[1:], tile_sem.at[0], tile_sem.at[1], partner)
     got_tiles[grp] = tiles[grp]
-    for i in reversed(range(n_grp - 1)):
-        tile_copy(i).wait_recv()
+    before = list(ends)
+    ends.clear()
+    send_all([tile_copy(o) for o in away], tiles_whole)
+    for copy in before:
+        copy.wait_send()
+    tiles_whole.wait_recv()
 
     field = jnp.concatenate([got_tiles[g] for g in range(n_grp)], axis=1)
     field_high = field.astype(BF16).astype(F32)
@@ -400,14 +433,14 @@
     def energy_copy(i):
         target = to(away[i])
         return remote(
-            energy.at[target], got_energy.at[i], en_send.at[i], en_recv.at[i], device(chip, core, target)
-        )
-
+            energy.at[target], got_energy.at[i], energy_sem.at[0], energy_sem.at[1], device(chip, core, target)
+        )
+
+    energy_whole = remote(energy.at[1:], got_energy.at[: n_grp - 1], energy_sem.at[0], energy_sem.at[1], partner)
+    send_all([energy_copy(i) for i in range(n_grp - 1)], energy_whole)
+    image = energy[grp]
+    energy_whole.wait_recv()
     for i in range(n_grp - 1):
-        send(energy_copy(i))
-    image = energy[grp]
-    for i in reversed(range(n_grp - 1)):
-        energy_copy(i).wait_recv()
         image += got_energy[i]
     n_windows = windows * n_win
     scale = 1.0 / (n_src * grid_x * GY * n_windows * n_windows)
@@ -417,8 +450,7 @@
         out[2 * p : 2 * p + 1] = jnp.where(low, one, pltpu.roll(two, GY, 1))
         out[2 * p + 1 : 2 * p + 2] = jnp.where(low, pltpu.roll(one, GY, 1), two)
 
-    for copy in sends:
-        copy.wait_send()
+    drain()
 
 
 def body(n_grp, n_win, spectra, freq_bins, slowness, positions):
@@ -457,10 +489,10 @@
             pltpu.VMEM((2 * LANES, receivers), BF16),
             pltpu.VMEM((grid_x, receivers), BF16),
             pltpu.VMEM((4, 2, grid_x, LANES), F32),
-            dma((5 + len(consts),)), dma((4,)),
-            dma((n_chunk, n_z)), dma((n_chunk, n_z)), dma((n_chunk, N_X)), dma((n_chunk, N_X)),
+            dma((5 + len(consts),)), dma((2,)), dma((n_chunk,)), dma((n_chunk,)),
+            dma((n_chunk, 2)), dma((n_chunk, 2)), dma((n_chunk,)), dma((n_chunk,)),
             dma((n_freq,)), dma((n_freq,)),
-            dma((n_grp,)), dma((n_grp,)), dma((n_grp,)), dma((n_grp,)),
+            dma((2,)), dma((2,)),
         ],
         compiler_params=pltpu.CompilerParams(
             collective_id=0, has_side_effects=True, vmem_limit_bytes=63 * 1024 * 1024

time: 57.4 us -> 53.1 us (0.925)
  the two profiles are of different devices: /device:TPU:6 before, /device:TPU:24 now
where the time goes in v4:
time: 53.1 us; the launch traced here: 52.9 us
  Pallas kernels  51.7 us (97%)
  local copies, waits for them, and re-layouts  1.26 us (2%)
    pallas_call x1, Pallas kernels, body(): pl.pallas_call(functools.partial(kernel, n_grp, n_win, windows), out_shap...  51.7 us
    unnamed x1, local copies, waits for them, and re-layouts  1.26 us

profile of v4, /device:TPU:24, one launch (start us, length us, event | category | flops | bytes accessed | tf_op | source)
XLA Modules:
  0.0 52.9 jit_solution(13084319652488588233)
XLA Ops:
  0.0 51.7 %shard_map.91 = f32[4,128]{1,0:T(4,128)} custom-call(bf16[16,2,256,128]{3,2,1,0:T(8,128)(2,1)} %bitcast.3, s32[1,2048]{1,0:T(1,128)} %bitcast.4, s32[32]{0:T(128)} %freq_hbm.1, f32[4]{0:T(128)} %slowness_hbm.1, bf16[2,128,64]{2,1,0:T(8,128)(2,1)} %constant.10.clone.rows_hbm, bf16[2,128,256]{2,1,0:T(8,128)(2,1)} %constant.11.clone.forward_hbm, ...), custom_call_target="tpu_custom_call" | custom-call | tf_op jit(solution)/shard_map/pallas_call | solution.py:468
  51.7 1.3 %copy.11 = f32[1,4,128]{2,1,0:T(4,128)} copy(f32[1,4,128]{2,1,0:T(4,128)} %bitcast.5) | data formatting | bytes 4096

commit v5 on v4

--- a/solution.py
+++ b/solution.py
@@ -44,7 +44,7 @@
 def coded(block):
     top = jnp.max(jnp.abs(block), axis=0, keepdims=True)
     exponent = jnp.ceil(jnp.log2(jnp.maximum(top, 1e-30)))
-    values = jnp.clip(jnp.round(block * (CODE_TOP * jnp.exp2(-exponent))), -CODE_TOP, CODE_TOP)
+    values = jnp.round(block * (CODE_TOP * jnp.exp2(-exponent)))
     return jnp.concatenate([values, jnp.broadcast_to(exponent, (EXTRA, LANES))], axis=0).astype(jnp.int32).astype(jnp.int16)
 
 
@@ -190,7 +190,8 @@
 
     barrier = pltpu.get_barrier_semaphore()
     greeted = [device(chip, core, to(o)) for o in away]
-    greeted += [device(at_y(d) * 2 + z, core, grp) for d in (2, -2, 1, -1) for z in range(2)]
+    greeted += [device(y * 2 + 1 - z_low, core, to(o)) for o in away]
+    greeted += [device(at_y(d) * 2 + z_low, core, grp) for d in (2, -2, 1, -1)]
     greeted += [device(y * 2 + 1 - z_low, core, grp), partner]
     greeted += [device(chip, other, to(o)) for o in away if 0 in o]
     for target in greeted:
@@ -221,7 +222,7 @@
 
     pl.semaphore_wait(barrier, len(greeted))
 
-    mixed = n_chunk - 2
+    mixed = n_chunk - 1
 
     def first_copy(c, axis, d, to_core):
         peer = to((d, 0) if axis == 0 else (0, d))
@@ -313,7 +314,6 @@
         for half in range(2):
             plain = dot(reorder, picked[c, :, :, half].reshape(height, rows)).astype(BF16)
             sources.append((plain, dot(plain, turn).astype(BF16)))
-        first_here = None
         for i in range(chunk):
             slot = chunk * c + i
             q = freq_of(slot)
@@ -328,21 +328,13 @@
                     result += block_arrived(slots.index((abs(passed) if passed == -4 else passed, z)))
             if d:
                 block_send(slot, result)
-            elif z == 0:
-                first_here = result
             else:
-                here = z_low == 0
-                own_gram[...] = jnp.where(here, first_here, result)
-                block_send(slot, jnp.where(here, result, first_here))
+                own_gram[z] = result
 
     def block_copy(slot):
         d, z = slots[slot]
-        if abs(d) > 2:
-            step = (2 if z == 0 else -2) if d == 4 else d // 3
-            target, index = at_y(step) * 2 + z_low, slot
-        else:
-            target = at_y(d) * 2 + (z if d else 1 - z_low)
-            index = slot - slot % 2 + z_low
+        step = ((2 if z == 0 else -2) if d == 4 else d // 3) if abs(d) > 2 else d
+        target, index = at_y(step) * 2 + z_low, slot
         return remote(
             blocks.at[slot], got_blocks.at[index], rs_send.at[slot], rs_recv.at[index], device(target, core, grp)
         )
@@ -357,44 +349,50 @@
         ).wait_recv()
         return decoded(got_blocks[index])
 
-    side_tables()
     for c in early:
         pick_copies[c].wait_recv()
         first_whole(c, 0 if c == mixed else 1).wait_recv()
         second_start(c)
+    side_tables()
     core_copy.wait_recv()
     for c in range(n_chunk):
         second_wait(c)
         grams(c)
-    total = own_gram[...]
-    for index in range(6, n_freq - 2):
-        total += block_arrived(index)
-    total += block_arrived(n_freq - 1 - z_low)
-
+    totals = []
+    for z in range(2):
+        total = own_gram[z]
+        for d in (2, 1, -2, -1):
+            total += block_arrived(slots.index((d, z)))
+        totals.append(total)
+
+    here = z_low == 0
     upper = lax.rem(iota((n_src, LANES), 0), 8) < SHOTS
-    real, imag = total[:n_src], total[n_src:]
-    first = jnp.where(upper, real, pltpu.roll(imag, SHOTS, 0))
-    second = jnp.where(upper, pltpu.roll(real, n_src - SHOTS, 0), imag)
-    for a in range(n_grp // 2):
-        tiles[2 * a] = first[8 * a : 8 * a + 8]
-        tiles[2 * a + 1] = second[8 * a : 8 * a + 8]
-
-    def tile_copy(offset):
+    for kind, total in enumerate((jnp.where(here, totals[0], totals[1]), jnp.where(here, totals[1], totals[0]))):
+        real, imag = total[:n_src], total[n_src:]
+        first = jnp.where(upper, real, pltpu.roll(imag, SHOTS, 0))
+        second = jnp.where(upper, pltpu.roll(real, n_src - SHOTS, 0), imag)
+        for a in range(n_grp // 2):
+            tiles[kind * n_grp + 2 * a] = first[8 * a : 8 * a + 8]
+            tiles[kind * n_grp + 2 * a + 1] = second[8 * a : 8 * a + 8]
+
+    def tile_copy(kind, offset):
         target = to(offset)
+        z = z_low if kind == 0 else 1 - z_low
         return remote(
-            tiles.at[target], got_tiles.at[grp], tile_sem.at[0], tile_sem.at[1], device(chip, core, target)
+            tiles.at[kind * n_grp + target], got_tiles.at[kind * n_grp + grp], tile_sem.at[0], tile_sem.at[1],
+            device(y * 2 + z, core, target),
         )
 
     tiles_whole = remote(tiles.at[1:], got_tiles.at[1:], tile_sem.at[0], tile_sem.at[1], partner)
     got_tiles[grp] = tiles[grp]
     before = list(ends)
     ends.clear()
-    send_all([tile_copy(o) for o in away], tiles_whole)
+    send_all([tile_copy(kind, o) for o in offsets for kind in (0, 1) if kind or o != (0, 0)], tiles_whole)
     for copy in before:
         copy.wait_send()
     tiles_whole.wait_recv()
 
-    field = jnp.concatenate([got_tiles[g] for g in range(n_grp)], axis=1)
+    field = jnp.concatenate([got_tiles[g] + got_tiles[n_grp + g] for g in range(n_grp)], axis=1)
     field_high = field.astype(BF16).astype(F32)
     field_low = field - field_high
     mask = x_mask[...]
@@ -479,11 +477,11 @@
             pltpu.VMEM((n_freq, rows, block), BF16),
             pltpu.VMEM((n_chunk, N_X, n_z, 2, 16, rows), BF16),
             pltpu.VMEM((n_chunk, 16, rows), BF16),
-            pltpu.VMEM((2 * n_src, block), F32),
+            pltpu.VMEM((2, 2 * n_src, block), F32),
             pltpu.VMEM((n_freq, 2 * n_src + EXTRA, block), jnp.int16),
             pltpu.VMEM((n_freq, 2 * n_src + EXTRA, block), jnp.int16),
-            pltpu.VMEM((n_grp, 2 * SHOTS, block), F32),
-            pltpu.VMEM((n_grp, 2 * SHOTS, block), F32),
+            pltpu.VMEM((2 * n_grp, 2 * SHOTS, block), F32),
+            pltpu.VMEM((2 * n_grp, 2 * SHOTS, block), F32),
             pltpu.VMEM((n_grp, SHOTS, block), F32),
             pltpu.VMEM((n_grp, SHOTS, block), F32),
             pltpu.VMEM((2 * LANES, receivers), BF16),

time: 53.1 us -> 52.8 us (level)
  the two profiles are of different devices: /device:TPU:24 before, /device:TPU:16 now
where the time goes in v5:
time: 52.8 us; the launch traced here: 52.7 us
  Pallas kernels  51.4 us (97%)
  local copies, waits for them, and re-layouts  1.26 us (2%)
    pallas_call x1, Pallas kernels, body(): pl.pallas_call(functools.partial(kernel, n_grp, n_win, windows), out_shap...  51.4 us
    unnamed x1, local copies, waits for them, and re-layouts  1.26 us

profile of v5, /device:TPU:16, one launch (start us, length us, event | category | flops | bytes accessed | tf_op | source)
XLA Modules:
  0.0 52.7 jit_solution(3634274785568280064)
XLA Ops:
  0.0 51.4 %shard_map.91 = f32[4,128]{1,0:T(4,128)} custom-call(bf16[16,2,256,128]{3,2,1,0:T(8,128)(2,1)} %bitcast.3, s32[1,2048]{1,0:T(1,128)} %bitcast.4, s32[32]{0:T(128)} %freq_hbm.1, f32[4]{0:T(128)} %slowness_hbm.1, bf16[2,128,64]{2,1,0:T(8,128)(2,1)} %constant.10.clone.rows_hbm, bf16[2,128,256]{2,1,0:T(8,128)(2,1)} %constant.11.clone.forward_hbm, ...), custom_call_target="tpu_custom_call" | custom-call | tf_op jit(solution)/shard_map/pallas_call | solution.py:466
  51.4 1.3 %copy.11 = f32[1,4,128]{2,1,0:T(4,128)} copy(f32[1,4,128]{2,1,0:T(4,128)} %bitcast.5) | data formatting | bytes 4096
